TPU v7x, 32 devices: a whole 2x2x4 slice. The times are simulated.
32 devices in a mesh: seq: 32 (over z, y, x, core).
Axes of the slice: x: 2, y: 2, z: 4, core: 2. Of those that a mesh axis runs over, the one named last changes fastest.
Arguments:
- hidden: bfloat16 [16384, 1472], P('seq'), may hold values from -6 to 6
- segments: int32 [16384], P('seq'), may hold values from 0 to 63, never falling along the last dimension, each value on 1 to 1024 neighbouring positions
- delete_mask: bfloat16 [16384], P('seq'), may hold values from -4 to 0
- bucket_table: int32 [2047], replicated, may hold values from 0 to 31
- attn_weight: bfloat16 [1472, 1536], P(None, 'seq'), may hold values from -1.1 to 1.1
- gate_weight: bfloat16 [1472, 3584], P(None, 'seq'), may hold values from -0.15625 to 0.15625
- up_weight: bfloat16 [1472, 3584], P(None, 'seq'), may hold values from -0.15625 to 0.15625
- down_weight: bfloat16 [3584, 1472], P('seq'), may hold values from -0.09375 to 0.09375
- norm_attn: float32 [1472], replicated, may hold values from 0.5 to 1.5
- norm_ffn: float32 [1472], replicated, may hold values from 0.5 to 1.5
- rel_bias: float32 [32, 6], replicated, may hold values from -4 to 4
- out_grad: bfloat16 [16384, 1472], P('seq'), may hold values from -6 to 6
Outputs:
- output: bfloat16 [16384, 1472], P('seq')
- d_hidden: float32 [16384, 1472], P('seq')
- d_attn_weight: float32 [1472, 1536], P(None, 'seq')
- d_gate_weight: float32 [1472, 3584], P(None, 'seq')
- d_up_weight: float32 [1472, 3584], P(None, 'seq')
- d_down_weight: float32 [3584, 1472], P('seq')
- d_norm_attn: float32 [1472], replicated
- d_norm_ffn: float32 [1472], replicated
- d_rel_bias: float32 [32, 6], replicated
Inputs may be any that keep to these rules, and one draw needn't show every extreme that they name: `segments`: tokens of one sequence are contiguous; sequence numbers never fall; each sequence holds 1 to 1024 tokens and one holds exactly 1024.
All inputs are finite; a program needn't handle non-finite values.
Results may differ from a plain program's by a relative error of at most 0.014.
The roundings to bfloat16 on the way count: a program that leaves them out, or rounds other values in their place, can miss the bound.
Values may be sent and summed in bfloat16 or wider, within the bound.
A program may use at most 320 MiB of HBM per device.

v0:
```python
import jax
import jax.numpy as jnp
from jax import lax
from jax.sharding import PartitionSpec as P


def shifted(x, axis, by):
    count = lax.axis_size(axis)
    pairs = [(i, i + by) for i in range(count) if 0 <= i + by < count]
    return lax.ppermute(x, axis, pairs)


def shortened(x):

    def short(part):
        return part.astype(jnp.bfloat16) if part.dtype == jnp.float32 else part

    return jax.tree.map(short, x)


def rms_norm(value, gain):
    return value * lax.rsqrt(jnp.mean(value * value, axis=-1, keepdims=True) + 1e-06) * gain


def matmul(left, right):
    return jnp.dot(left, right, preferred_element_type=jnp.float32)


def matmul_tn(left, right):
    return lax.dot_general(
        left, right, (((0,), (0,)), ((), ())), preferred_element_type=jnp.float32
    )


def matmul_nt(left, right):
    return lax.dot_general(
        left, right, (((1,), (1,)), ((), ())), preferred_element_type=jnp.float32
    )


def gated_unit(gate_in, up_in):
    return jax.nn.gelu(gate_in) * up_in


def toeplitz(line, row_count, window):
    span_len = line.shape[0]
    tiled = jnp.tile(line, row_count)[: row_count * (span_len - 1)].reshape(row_count, span_len - 1)
    return tiled[:, :window]


def diagonal_sums(plane, span_len):
    row_count, window = plane.shape
    padded = jnp.pad(plane, ((0, 0), (0, span_len - 1 - window))).reshape(-1)
    padded = jnp.pad(padded, (0, row_count)).reshape(row_count, span_len)
    return jnp.sum(padded, axis=0)


def head_scores(q_head, k_head, mask_win, same_doc, bias_plane):
    raw = matmul_nt(q_head, k_head)
    scores = raw + bias_plane + mask_win[None, :]
    return jnp.where(same_doc, scores, -1e30)


def shards(
    hidden,
    segments,
    delete_mask,
    bucket_table,
    attn_weight,
    gate_weight,
    up_weight,
    down_weight,
    norm_attn,
    norm_ffn,
    rel_bias,
    out_grad,
):
    row_count = hidden.shape[0]
    head_count = rel_bias.shape[1]
    bucket_count = rel_bias.shape[0]
    inner_width = attn_weight.shape[1] * lax.axis_size("seq") // 4
    head_width = inner_width // head_count
    table_len = bucket_table.shape[0]
    longest = (table_len + 1) // 2
    reach_blocks = (longest + row_count - 2) // row_count
    margin = reach_blocks * row_count
    window = (2 * reach_blocks + 1) * row_count
    span_len = row_count + window - 1
    w_attn, w_gate, w_up, w_down = (
        lax.all_gather(attn_weight, "seq", axis=1, tiled=True),
        lax.all_gather(gate_weight, "seq", axis=1, tiled=True),
        lax.all_gather(up_weight, "seq", axis=1, tiled=True),
        lax.all_gather(down_weight, "seq", axis=0, tiled=True),
    )
    residual = hidden.astype(jnp.float32)
    normed = rms_norm(residual, norm_attn).astype(jnp.bfloat16)
    projected = matmul(normed, w_attn[:, : 3 * inner_width]).astype(jnp.bfloat16)
    queries = projected[:, :inner_width]
    key_rows = projected[:, inner_width : 2 * inner_width]
    value_rows = projected[:, 2 * inner_width :]
    own_block = (key_rows, value_rows, segments + 1, delete_mask)
    both_sides = []
    for direction in (1, -1):
        current = own_block
        received = []
        for distance in range(reach_blocks):
            current = shifted((current[0], current[1], current[2], current[3]), "seq", direction)
            received.append(current)
        both_sides.append(received)
    ordered = both_sides[0][::-1] + [own_block] + both_sides[1]
    k_win = jnp.concatenate([portion[0] for portion in ordered], 0)
    v_win = jnp.concatenate([portion[1] for portion in ordered], 0)
    seg_win = jnp.concatenate([portion[2] for portion in ordered], 0)
    mask_win = jnp.concatenate([portion[3] for portion in ordered], 0).astype(jnp.float32)
    line_index = (jnp.arange(span_len, dtype=jnp.int32) + row_count - 1) % span_len
    line_offset = line_index - margin - (row_count - 1)
    line_bucket = jnp.take(
        bucket_table, jnp.clip(line_offset, 1 - longest, longest - 1) + longest - 1
    )
    line_onehot = (
        line_bucket[:, None] == jnp.arange(bucket_count, dtype=jnp.int32)[None, :]
    ).astype(jnp.float32)
    line_bias = jnp.dot(line_onehot, rel_bias, precision=lax.Precision.HIGHEST)
    same_doc = segments[:, None] + 1 == seg_win[None, :]
    mixed_parts = []
    log_parts = []
    for head in range(head_count):
        cols = slice(head * head_width, (head + 1) * head_width)
        bias_plane = toeplitz(line_bias[:, head], row_count, window)
        scores = head_scores(queries[:, cols], k_win[:, cols], mask_win, same_doc, bias_plane)
        row_max = jnp.max(scores, axis=-1, keepdims=True)
        exp_scores = jnp.exp(scores - row_max)
        row_total = jnp.sum(exp_scores, axis=-1, keepdims=True)
        log_parts.append(row_max + jnp.log(row_total))
        softmax_weights = (exp_scores / row_total).astype(jnp.bfloat16)
        mixed_parts.append(matmul(softmax_weights, v_win[:, cols]))
    attended = jnp.concatenate(mixed_parts, 1).astype(jnp.bfloat16)
    w_out = w_attn[:, 3 * inner_width :]
    after = residual + matmul_nt(attended, w_out)
    normed_ffn = rms_norm(after, norm_ffn).astype(jnp.bfloat16)
    gate_act = matmul(normed_ffn, w_gate)
    up_act = matmul(normed_ffn, w_up)
    activated = gated_unit(gate_act, up_act).astype(jnp.bfloat16)
    output = (after + matmul(activated, w_down)).astype(jnp.bfloat16)
    d_activated = matmul_nt(out_grad, w_down)
    d_down = matmul_tn(activated, out_grad)
    unit_out, unit_pull = jax.vjp(gated_unit, gate_act, up_act)
    d_gate_act, d_up_act = unit_pull(d_activated)
    d_gate_act = d_gate_act.astype(jnp.bfloat16)
    d_up_act = d_up_act.astype(jnp.bfloat16)
    d_normed_ffn = matmul_nt(d_gate_act, w_gate) + matmul_nt(d_up_act, w_up)
    d_w_gate = matmul_tn(normed_ffn, d_gate_act)
    d_w_up = matmul_tn(normed_ffn, d_up_act)
    norm_out, second_pull = jax.vjp(rms_norm, after, norm_ffn)
    d_after_part, d_norm_ffn = second_pull(d_normed_ffn)
    d_after = out_grad.astype(jnp.float32) + d_after_part
    d_after_low = d_after.astype(jnp.bfloat16)
    d_w_out = matmul_tn(d_after_low, attended)
    d_mixed = matmul(d_after_low, w_out).astype(jnp.bfloat16)
    dq_parts = []
    dk_parts = []
    dv_parts = []
    line_grads = []
    for head in range(head_count):
        cols = slice(head * head_width, (head + 1) * head_width)
        bias_plane = toeplitz(line_bias[:, head], row_count, window)
        scores = head_scores(queries[:, cols], k_win[:, cols], mask_win, same_doc, bias_plane)
        recomputed = jnp.exp(scores - log_parts[head])
        d_mix_head = d_mixed[:, cols]
        d_weights = matmul_nt(d_mix_head, v_win[:, cols])
        dv_parts.append(matmul_tn(recomputed.astype(jnp.bfloat16), d_mix_head))
        row_delta = jnp.sum(recomputed * d_weights, axis=-1, keepdims=True)
        d_scores = recomputed * (d_weights - row_delta)
        line_grads.append(diagonal_sums(d_scores, span_len))
        d_scores_low = d_scores.astype(jnp.bfloat16)
        dq_parts.append(matmul(d_scores_low, k_win[:, cols]))
        dk_parts.append(matmul_tn(d_scores_low, queries[:, cols]))
    d_queries = jnp.concatenate(dq_parts, 1)
    d_k_win = jnp.concatenate(dk_parts, 1)
    d_v_win = jnp.concatenate(dv_parts, 1)
    d_rel = lax.dot_general(
        line_onehot,
        jnp.stack(line_grads, 1),
        (((0,), (0,)), ((), ())),
        precision=lax.Precision.HIGHEST,
    )
    returned = [
        (
            d_k_win[slot * row_count : (slot + 1) * row_count],
            d_v_win[slot * row_count : (slot + 1) * row_count],
        )
        for slot in range(2 * reach_blocks + 1)
    ]
    d_keys = returned[reach_blocks][0]
    d_values = returned[reach_blocks][1]
    for direction in (1, -1):
        carried = (jnp.zeros_like(d_keys), jnp.zeros_like(d_values))
        for distance in range(reach_blocks, 0, -1):
            portion = returned[reach_blocks - direction * distance]
            carried = shifted(
                (shortened(carried[0] + portion[0]), shortened(carried[1] + portion[1])),
                "seq",
                -direction,
            )
        d_keys = d_keys + carried[0]
        d_values = d_values + carried[1]
    d_projected = jnp.concatenate([d_queries, d_keys, d_values], 1).astype(jnp.bfloat16)
    d_normed = matmul_nt(d_projected, w_attn[:, : 3 * inner_width])
    d_w_proj = matmul_tn(normed, d_projected)
    first_out, first_pull = jax.vjp(rms_norm, residual, norm_attn)
    d_resid_part, d_norm_attn = first_pull(d_normed)
    d_hidden = d_after + d_resid_part
    d_attn_full = jnp.concatenate([d_w_proj, d_w_out], 1)
    g_attn, g_gate, g_up, g_down = (
        lax.psum_scatter(d_attn_full, "seq", scatter_dimension=1, tiled=True),
        lax.psum_scatter(d_w_gate, "seq", scatter_dimension=1, tiled=True),
        lax.psum_scatter(d_w_up, "seq", scatter_dimension=1, tiled=True),
        lax.psum_scatter(d_down, "seq", scatter_dimension=0, tiled=True),
    )
    s_attn, s_ffn, s_rel = lax.psum((d_norm_attn, d_norm_ffn, d_rel), "seq")
    return (output, d_hidden, g_attn, g_gate, g_up, g_down, s_attn, s_ffn, s_rel)


def solution(mesh):
    placed = (
        P("seq", None),
        P("seq"),
        P("seq"),
        P(),
        P(None, "seq"),
        P(None, "seq"),
        P(None, "seq"),
        P("seq", None),
        P(),
        P(),
        P(),
        P("seq", None),
    )
    return jax.shard_map(
        shards,
        mesh=mesh,
        in_specs=placed,
        out_specs=(
            P("seq", None),
            P("seq", None),
            P(None, "seq"),
            P(None, "seq"),
            P(None, "seq"),
            P("seq", None),
            P(),
            P(),
            P(),
        ),
        check_vma=False,
    )
```

profile of v0, /device:TPU:0, one launch (start us, length us, event | category | flops | bytes accessed | tf_op | source)
XLA Modules:
  0.0 1428.8 jit_solution(4787005292600462845)
XLA Ops:
  15.7 5.8 collective-permute-start
  21.6 17.4 %gather_fusion = s32[3071]{0:T(1024)S(1)} fusion(s32[2047]{0:T(1024)S(1)} %copy-done, s32[3072]{0:T(1024)S(1)} %pad_clamp_fusion), kind=kCustom, calls=%fused_computation | custom fusion | bytes 36852 | tf_op jit(solution)/shard_map/jit(_take)/gather | solution.py:117
  39.7 37.6 %all-gather.5.cloned.1.call-done = bf16[1472,1536]{0,1:T(8,128)(2,1)} async-done(((bf16[1472,48]{0,1:T(8,128)(2,1)}), bf16[1472,1536]{0,1:T(8,128)(2,1)}) %all-gather.5.cloned.1.call-update) | async-done | bytes 4522000 | tf_op jit(solution)/shard_map/all_gather | solution.py:90
  87.7 8.9 tile.98
  101.5 9.5 reshape.289
  114.4 8.8 tile.101
  123.2 5.1 slice.322
  128.3 9.7 reshape.290
  141.5 8.8 tile.47
  155.1 9.5 reshape.288
  172.3 8.9 tile.44
  186.0 9.6 reshape.287
  200.3 8.9 tile.41
  209.2 5.1 slice.298
  214.4 9.5 reshape.286
  227.3 8.9 tile.38
  240.9 9.5 reshape.285
  274.2 6.4 collective-permute-done.15
  280.7 7.9 collective-permute-done.7
  311.0 5.1 fusion.214
  331.9 11.5 fusion.221
  343.4 11.2 fusion.220
  357.6 19.8 %multiply_convert_fusion = (bf16[512,3584]{1,0:T(8,128)(2,1)}, bf16[512,3584]{1,0:T(8,128)(2,1)}, bf16[512,3584]{1,0:T(8,128)(2,1)}) fusion(f32[512,3584]{1,0:T(8,128)} %fusion.220, f32[512,3584]{1,0:T(8,128)} %fusion.221, bf16[512,1472]{0,1:T(8,128)(2,1)} %param.23, bf16[3584,1472]{1,0:T(8,128)(2,1)} %all-gather.11.cloned.1.call-done), kind=kOutput, calls=%fused_computation.17 | convolution fusion | flops 5449973760 | bytes 37748736 | tf_op jit(solution)/shard_map/dot_general | solution.py:36
  377.4 14.7 %fusion.222 = f32[512,1472]{0,1:T(8,128)} fusion(bf16[512,3584]{1,0:T(8,128)(2,1)} %get-tuple-element.53, bf16[1472,3584]{0,1:T(8,128)(2,1)} %all-gather.7.cloned.1.call-done), kind=kOutput, calls=%fused_computation.304 | convolution fusion | flops 5402263552 | bytes 17235968 | tf_op jit(solution)/shard_map/dot_general | solution.py:36
  392.2 16.6 %multiply_reduce_fusion.6 = (f32[1472]{0:T(1024)}, f32[512]{0:T(512)S(1)}, f32[512,1472]{0,1:T(8,128)}) fusion(f32[512,1472]{0,1:T(8,128)S(1)} %get-tuple-element.86, f32[512]{0:T(512)S(1)} %fusion.209, f32[1472]{0:T(1024)S(1)} %copy-done.40, f32[512,1472]{0,1:T(8,128)} %fusion.222, bf16[512,3584]{1,0:T(8,128)(2,1)} %get-tuple-element.52, ...), kind=kOutput, calls=%fused_computation.107 | convolution fusion | flops 5407537152 | bytes 23281152 | tf_op jit(solution)/shard_map/dot_general | solution.py:36
  456.5 19.4 %collective-permute-start.22 = (bf16[512,384]{0,1:T(8,128)(2,1)}, bf16[512,384]{0,1:T(8,128)(2,1)}, u32[]{:S(2)}, u32[]{:S(2)}) collective-permute-start(bf16[512,384]{0,1:T(8,128)(2,1)} %get-tuple-element.60), channel_id=1, source_target_pairs={{0,1},{1,2},{2,3},{3,4},{4,5},{5,6},{6,7},{7,8},{8,9},{9,10},{10,1... | collective-permute-start | bytes 1179656 | tf_op jit(solution)/shard_map/ppermute | solution.py:10
  475.9 7.6 subtract_multiply_fusion.4
  490.6 5.9 subtract_multiply_fusion.3
  516.2 5.5 subtract_multiply_fusion.1
  539.7 9.3 collective-permute-start.19
  551.9 5.0 collective-permute-start.23
  560.6 4.9 fusion.168
  565.5 7.7 pad_maximum_fusion
  573.3 9.5 copy.25
  584.1 12.8 fusion.225
  598.4 13.3 fusion.224
  611.9 13.4 fusion.223
  625.3 6.4 pad.48
  631.8 6.3 pad.46
  652.3 9.5 reshape.301
  661.8 5.0 pad.49
  666.9 9.6 reshape.302
  679.6 9.5 reshape.299
  689.1 4.9 pad.47
  694.0 9.4 reshape.300
  706.6 9.4 reshape.297
  716.0 5.2 pad.45
  721.2 9.4 reshape.298
  733.7 9.7 reshape.295
  743.3 5.6 pad.43
  748.9 10.1 reshape.296
  762.6 10.2 reshape.293
  772.8 5.4 pad.41
  778.2 9.9 reshape.294
  791.2 9.5 reshape.291
  800.7 5.0 pad.39
  805.8 9.4 reshape.292
  819.1 14.7 %fusion.40 = bf16[512,1472]{0,1:T(8,128)(2,1)} fusion(f32[512,1472]{0,1:T(8,128)S(1)} %copy-done.17, bf16[512,3584]{1,0:T(8,128)(2,1)} %get-tuple-element.54, bf16[3584,1472]{1,0:T(8,128)(2,1)} %all-gather.11.cloned.1.call-done), kind=kOutput, calls=%fused_computation.112 | convolution fusion | flops 5403770880 | bytes 18743296 | tf_op jit(solution)/shard_map/dot_general | solution.py:26
  833.9 6.5 fusion.32
  840.4 50.0 %all-reduce.12 = (f32[1472]{0:T(1024)}, f32[1472]{0:T(1024)}, f32[32,6]{0,1:T(8,128)}) all-reduce(f32[1472]{0:T(1024)S(1)} %get-tuple-element.47, f32[1472]{0:T(1024)S(1)} %copy-done.43, f32[32,6]{0,1:T(8,128)S(1)} %fusion.173), channel_id=1, replica_groups=mesh['seq'=32] {'seq'}, use_global_device_ids=true, to_apply=%region_27.28 | all-reduce | flops 3136 | bytes 25088 | tf_op jit(solution)/shard_map/psum | solution.py:220
  890.4 5.5 fusion.34
  895.9 62.2 %reduce-scatter.11.cloned.1.call-done = f32[112,1472]{1,0:T(8,128)} async-done(((f32[3584,1472]{1,0:T(8,128)}), f32[112,1472]{1,0:T(8,128)}) %reduce-scatter.11.cloned.1.call-update) | async-done | bytes 659472 | tf_op jit(solution)/shard_map/reduce_scatter | solution.py:218
  958.1 231.7 %reduce-scatter.9.cloned.1.call-done = f32[1472,112]{0,1:T(8,128)} async-done(((f32[1472,3584]{0,1:T(8,128)}), f32[1472,112]{0,1:T(8,128)}) %reduce-scatter.9.cloned.1.call-update) | async-done | bytes 659472 | tf_op jit(solution)/shard_map/reduce_scatter | solution.py:217
  1189.8 231.7 %reduce-scatter.7.cloned.1.call-done = f32[1472,112]{0,1:T(8,128)} async-done(((f32[1472,3584]{0,1:T(8,128)}), f32[1472,112]{0,1:T(8,128)}) %reduce-scatter.7.cloned.1.call-update) | async-done | bytes 659472 | tf_op jit(solution)/shard_map/reduce_scatter | solution.py:216
  (364 shorter events, 261.8 us)
Async XLA Ops:
  7.2 14.4 %copy-start = (s32[2047]{0:T(1024)S(1)}, s32[2047]{0:T(1024)}, u32[]{:S(2)}) copy-start(s32[2047]{0:T(1024)} %param.15) | copy-start | bytes 24568
  7.2 70.1 %all-gather.5.cloned.1.call-start = ((), (), s32[]{:S(2)}) async-start(), calls=%async_computation.4 | async-start | bytes 4866048 | tf_op jit(solution)/shard_map/all_gather | solution.py:90
  7.9 324.0 %all-gather.9.cloned.1.call-start = ((), (), s32[]{:S(2)}) async-start(), calls=%async_computation.6 | async-start | bytes 11354112 | tf_op jit(solution)/shard_map/all_gather | solution.py:92
  8.7 334.8 %all-gather.7.cloned.1.call-start = ((), (), s32[]{:S(2)}) async-start(), calls=%async_computation.5 | async-start | bytes 11354112 | tf_op jit(solution)/shard_map/all_gather | solution.py:91
  9.4 348.2 %all-gather.11.cloned.1.call-start = ((), (), s32[]{:S(2)}) async-start(), calls=%async_computation.7 | async-start | bytes 11354112 | tf_op jit(solution)/shard_map/all_gather | solution.py:93
  10.0 885.9 %reduce-scatter.13.cloned.1.call-start = ((), (), s32[]{:S(2)}) async-start(), calls=%async_computation.11 | async-start | bytes 9732096
  10.0 154.5 %collective-permute-start.8 = (bf16[512]{0:T(512)(128)(2,1)}, bf16[512]{0:T(512)(128)(2,1)S(1)}, u32[]{:S(2)}, u32[]{:S(2)}) collective-permute-start(bf16[512]{0:T(512)(128)(2,1)} %param.14), channel_id=1, source_target_pairs={{0,1},{1,2},{2,3},{3,4},{4,5},{5,6},{6,7},{7,8},{8,9},{9,10},{10,1... | collective-permute-start | bytes 3080 | tf_op jit(solution)/shard_map/ppermute | solution.py:10
  12.4 183.2 %collective-permute-start.10 = (bf16[512]{0:T(512)(128)(2,1)}, bf16[512]{0:T(512)(128)(2,1)S(1)}, u32[]{:S(2)}, u32[]{:S(2)}) collective-permute-start(bf16[512]{0:T(512)(128)(2,1)} %param.14), channel_id=1, source_target_pairs={{1,0},{2,1},{3,2},{4,3},{5,4},{6,5},{7,6},{8,7},{9,8},{10,9},{11,1... | collective-permute-start | bytes 3080 | tf_op jit(solution)/shard_map/ppermute | solution.py:10
  14.4 240.3 %collective-permute-start.2 = (s32[512]{0:T(512)S(1)}, s32[512]{0:T(512)S(1)}, u32[]{:S(2)}, u32[]{:S(2)}) collective-permute-start(s32[512]{0:T(512)S(1)} %broadcast_add_fusion), channel_id=1, source_target_pairs={{1,0},{2,1},{3,2},{4,3},{5,4},{6,5},{7,6},{8,7},{9,8},{10,9},{11,1... | collective-permute-start | bytes 6152 | tf_op jit(solution)/shard_map/ppermute | solution.py:10
  15.7 235.3 %collective-permute-start = (s32[512]{0:T(512)S(1)}, s32[512]{0:T(512)S(1)}, u32[]{:S(2)}, u32[]{:S(2)}) collective-permute-start(s32[512]{0:T(512)S(1)} %broadcast_add_fusion), channel_id=1, source_target_pairs={{0,1},{1,2},{2,3},{3,4},{4,5},{5,6},{6,7},{7,8},{8,9},{9,10},{10,1... | collective-permute-start | bytes 6152 | tf_op jit(solution)/shard_map/ppermute | solution.py:10
  21.6 17.5 %copy-start.20 = (bf16[512,1472]{0,1:T(8,128)(2,1)S(1)}, bf16[512,1472]{0,1:T(8,128)(2,1)}, u32[]{:S(2)}) copy-start(bf16[512,1472]{0,1:T(8,128)(2,1)} %param.12) | copy-start | bytes 4521988
  21.6 17.9 %copy-start.51 = (f32[32,6]{0,1:T(8,128)S(1)}, f32[32,6]{0,1:T(8,128)}, u32[]{:S(2)}) copy-start(f32[32,6]{0,1:T(8,128)} %param.22) | copy-start | bytes 2308
  21.6 55.7 %copy-start.45 = (f32[1472]{0:T(1024)S(1)}, f32[1472]{0:T(1024)}, u32[]{:S(2)}) copy-start(f32[1472]{0:T(1024)} %param.20) | copy-start | bytes 17668
  39.4 42.4 %copy-start.41 = (f32[512]{0:T(512)}, f32[512]{0:T(512)S(1)}, u32[]{:S(2)}) copy-start(f32[512]{0:T(512)S(1)} %fusion.35) | copy-start | bytes 6148
  39.4 42.4 %copy-start.48 = (f32[512]{0:T(512)}, f32[512]{0:T(512)S(1)}, u32[]{:S(2)}) copy-start(f32[512]{0:T(512)S(1)} %fusion.208) | copy-start | bytes 6148
  39.5 42.4 %copy-start.38 = (s32[3071]{0:T(1024)}, s32[3071]{0:T(1024)S(1)}, u32[]{:S(2)}) copy-start(s32[3071]{0:T(1024)S(1)} %and_select_fusion.1) | copy-start | bytes 36856
  81.9 214.7 %copy-start.30 = (bf16[512,1152]{1,0:T(8,128)(2,1)}, bf16[512,1152]{1,0:T(8,128)(2,1)S(1)}, u32[]{:S(2)}) copy-start(bf16[512,1152]{1,0:T(8,128)(2,1)S(1)} %fusion.37) | copy-start | bytes 3538948
  82.0 180.3 %collective-permute-start.4 = (bf16[512,384]{1,0:T(8,128)(2,1)S(1)}, bf16[512,384]{1,0:T(8,128)(2,1)S(1)}, u32[]{:S(2)}, u32[]{:S(2)}) collective-permute-start(bf16[512,384]{1,0:T(8,128)(2,1)S(1)} %get-tuple-element.66), channel_id=1, source_target_pairs={{0,1},{1,2},{2,3},{3,4},{4,5},{5,6},{6,7},{7,8},{8,9},{9,10},{10,1... | collective-permute-start | bytes 1179656 | tf_op jit(solution)/shard_map/ppermute | solution.py:10
  164.5 85.9 %collective-permute-start.9 = (bf16[512]{0:T(512)(128)(2,1)S(1)}, bf16[512]{0:T(512)(128)(2,1)S(1)}, u32[]{:S(2)}, u32[]{:S(2)}) collective-permute-start(bf16[512]{0:T(512)(128)(2,1)S(1)} %collective-permute-done.8), channel_id=1, source_target_pairs={{0,1},{1,2},{2,3},{3,4},{4,5},{5,6},{6,7},{7,8},{8,9},{9,10},{10,1... | collective-permute-start | bytes 3080 | tf_op jit(solution)/shard_map/ppermute | solution.py:10
  195.6 59.0 %collective-permute-start.11 = (bf16[512]{0:T(512)(128)(2,1)S(1)}, bf16[512]{0:T(512)(128)(2,1)S(1)}, u32[]{:S(2)}, u32[]{:S(2)}) collective-permute-start(bf16[512]{0:T(512)(128)(2,1)S(1)} %collective-permute-done.10), channel_id=1, source_target_pairs={{1,0},{2,1},{3,2},{4,3},{5,4},{6,5},{7,6},{8,7},{9,8},{10,9},{11,1... | collective-permute-start | bytes 3080 | tf_op jit(solution)/shard_map/ppermute | solution.py:10
  240.9 26.3 %copy-start.44 = (s32[512]{0:T(512)S(1)}, s32[512]{0:T(512)}, u32[]{:S(2)}) copy-start(s32[512]{0:T(512)} %param.13) | copy-start | bytes 6148
  251.0 8.6 collective-permute-start.1
  254.7 16.2 %collective-permute-start.3 = (s32[512]{0:T(512)S(1)}, s32[512]{0:T(512)S(1)}, u32[]{:S(2)}, u32[]{:S(2)}) collective-permute-start(s32[512]{0:T(512)S(1)} %collective-permute-done.2), channel_id=1, source_target_pairs={{1,0},{2,1},{3,2},{4,3},{5,4},{6,5},{7,6},{8,7},{9,8},{10,9},{11,1... | collective-permute-start | bytes 6152 | tf_op jit(solution)/shard_map/ppermute | solution.py:10
  256.0 11.2 collective-permute-start.12
  259.6 11.2 collective-permute-start.14
  260.9 11.2 collective-permute-start.6
  262.3 11.4 collective-permute-start.5
  267.2 6.6 collective-permute-start.13
  270.9 9.7 collective-permute-start.15
  272.2 16.4 %collective-permute-start.7 = (bf16[512,384]{1,0:T(8,128)(2,1)S(1)}, bf16[512,384]{1,0:T(8,128)(2,1)S(1)}, u32[]{:S(2)}, u32[]{:S(2)}) collective-permute-start(bf16[512,384]{1,0:T(8,128)(2,1)S(1)} %collective-permute-done.6), channel_id=1, source_target_pairs={{1,0},{2,1},{3,2},{4,3},{5,4},{6,5},{7,6},{8,7},{9,8},{10,9},{11,1... | collective-permute-start | bytes 1179656 | tf_op jit(solution)/shard_map/ppermute | solution.py:10
  288.7 22.3 %copy-start.18 = (bf16[2560,384]{1,0:T(8,128)(2,1)}, bf16[2560,384]{1,0:T(8,128)(2,1)S(1)}, u32[]{:S(2)}) copy-start(bf16[2560,384]{1,0:T(8,128)(2,1)S(1)} %constant_dynamic-update-slice_fusion.1) | copy-start | bytes 5898244
  293.3 31.3 %copy-start.2 = (f32[512,2560]{1,0:T(8,128)}, f32[512,2560]{1,0:T(8,128)S(1)}, u32[]{:S(2)}) copy-start(f32[512,2560]{1,0:T(8,128)S(1)} %get-tuple-element.82) | copy-start | bytes 15728644
  295.7 30.1 %copy-start.3 = (f32[512,2560]{1,0:T(8,128)}, f32[512,2560]{1,0:T(8,128)S(1)}, u32[]{:S(2)}) copy-start(f32[512,2560]{1,0:T(8,128)S(1)} %get-tuple-element.84) | copy-start | bytes 15728644
  301.4 21.7 %copy-start.4 = (f32[512,2560]{1,0:T(8,128)}, f32[512,2560]{1,0:T(8,128)S(1)}, u32[]{:S(2)}) copy-start(f32[512,2560]{1,0:T(8,128)S(1)} %get-tuple-element.80) | copy-start | bytes 15728644
  306.6 15.2 %copy-start.5 = (f32[512,2560]{1,0:T(8,128)}, f32[512,2560]{1,0:T(8,128)S(1)}, u32[]{:S(2)}) copy-start(f32[512,2560]{1,0:T(8,128)S(1)} %get-tuple-element.78) | copy-start | bytes 15728644
  310.1 10.2 copy-start.6
  329.9 62.3 %copy-start.16 = (f32[512,1472]{0,1:T(8,128)}, f32[512,1472]{0,1:T(8,128)S(1)}, u32[]{:S(2)}) copy-start(f32[512,1472]{0,1:T(8,128)S(1)} %get-tuple-element.86) | copy-start | bytes 9043972
  392.2 16.6 %copy-start.36 = (bf16[512,1472]{0,1:T(8,128)(2,1)S(1)}, bf16[512,1472]{0,1:T(8,128)(2,1)}, u32[]{:S(2)}) copy-start(bf16[512,1472]{0,1:T(8,128)(2,1)} %param.23) | copy-start | bytes 4521988
  412.5 144.5 %copy-start.14 = (f32[512,1472]{0,1:T(8,128)}, f32[512,1472]{0,1:T(8,128)S(1)}, u32[]{:S(2)}) copy-start(f32[512,1472]{0,1:T(8,128)S(1)} %fusion.33) | copy-start | bytes 9043972
  455.2 93.8 %collective-permute-start.20 = (bf16[512,384]{0,1:T(8,128)(2,1)}, bf16[512,384]{0,1:T(8,128)(2,1)}, u32[]{:S(2)}, u32[]{:S(2)}) collective-permute-start(bf16[512,384]{0,1:T(8,128)(2,1)} %get-tuple-element.59), channel_id=1, source_target_pairs={{1,0},{2,1},{3,2},{4,3},{5,4},{6,5},{7,6},{8,7},{9,8},{10,9},{11,1... | collective-permute-start | bytes 1179656 | tf_op jit(solution)/shard_map/ppermute | solution.py:10
  456.5 92.5 %collective-permute-start.22 = (bf16[512,384]{0,1:T(8,128)(2,1)}, bf16[512,384]{0,1:T(8,128)(2,1)}, u32[]{:S(2)}, u32[]{:S(2)}) collective-permute-start(bf16[512,384]{0,1:T(8,128)(2,1)} %get-tuple-element.60), channel_id=1, source_target_pairs={{0,1},{1,2},{2,3},{3,4},{4,5},{5,6},{6,7},{7,8},{8,9},{9,10},{10,1... | collective-permute-start | bytes 1179656 | tf_op jit(solution)/shard_map/ppermute | solution.py:10
  516.2 19.2 %copy-start.12 = (f32[512,2560]{1,0:T(8,128)}, f32[512,2560]{1,0:T(8,128)S(1)}, u32[]{:S(2)}) copy-start(f32[512,2560]{1,0:T(8,128)S(1)} %subtract_multiply_fusion) | copy-start | bytes 15728644
  521.6 12.8 copy-start.13
  529.2 7.4 collective-permute-start.16
  530.5 6.2 collective-permute-start.18
  535.4 13.6 copy-start.26
  535.4 21.6 %copy-start.34 = (bf16[512,384]{0,1:T(8,128)(2,1)S(1)}, bf16[512,384]{0,1:T(8,128)(2,1)}, u32[]{:S(2)}) copy-start(bf16[512,384]{0,1:T(8,128)(2,1)} %copy-done.33) | copy-start | bytes 1179652
  538.4 19.6 %collective-permute-start.17 = (bf16[512,384]{0,1:T(8,128)(2,1)S(1)}, bf16[512,384]{0,1:T(8,128)(2,1)S(1)}, u32[]{:S(2)}, u32[]{:S(2)}) collective-permute-start(bf16[512,384]{0,1:T(8,128)(2,1)S(1)} %get-tuple-element.57), channel_id=1, source_target_pairs={{1,0},{2,1},{3,2},{4,3},{5,4},{6,5},{7,6},{8,7},{9,8},{10,9},{11,1... | collective-permute-start | bytes 1179656 | tf_op jit(solution)/shard_map/ppermute | solution.py:10
  539.7 18.3 %collective-permute-start.19 = (bf16[512,384]{0,1:T(8,128)(2,1)S(1)}, bf16[512,384]{0,1:T(8,128)(2,1)S(1)}, u32[]{:S(2)}, u32[]{:S(2)}) collective-permute-start(bf16[512,384]{0,1:T(8,128)(2,1)S(1)} %get-tuple-element.58), channel_id=1, source_target_pairs={{0,1},{1,2},{2,3},{3,4},{4,5},{5,6},{6,7},{7,8},{8,9},{9,10},{10,1... | collective-permute-start | bytes 1179656 | tf_op jit(solution)/shard_map/ppermute | solution.py:10
  550.5 8.8 collective-permute-start.21
  551.9 7.4 collective-permute-start.23
  582.8 375.3 %reduce-scatter.11.cloned.1.call-start = ((), (), s32[]{:S(2)}) async-start(), calls=%async_computation.10 | async-start | bytes 22708224 | tf_op jit(solution)/shard_map/reduce_scatter | solution.py:218
  596.9 592.9 %reduce-scatter.9.cloned.1.call-start = ((), (), s32[]{:S(2)}) async-start(), calls=%async_computation.9 | async-start | bytes 22708224 | tf_op jit(solution)/shard_map/reduce_scatter | solution.py:217
  611.7 809.8 %reduce-scatter.7.cloned.1.call-start = ((), (), s32[]{:S(2)}) async-start(), calls=%async_computation.8 | async-start | bytes 22708224 | tf_op jit(solution)/shard_map/reduce_scatter | solution.py:216
  625.3 12.7 slice-start.18
  625.3 12.7 slice-start.19
  631.8 13.7 slice-start.14
  819.1 14.7 %copy-start.23 = (bf16[512,1472]{0,1:T(8,128)(2,1)S(1)}, bf16[512,1472]{0,1:T(8,128)(2,1)}, u32[]{:S(2)}) copy-start(bf16[512,1472]{0,1:T(8,128)(2,1)} %param.12) | copy-start | bytes 4521988
  819.1 14.8 %copy-start.47 = (f32[1472]{0:T(1024)S(1)}, f32[1472]{0:T(1024)}, u32[]{:S(2)}) copy-start(f32[1472]{0:T(1024)} %param.20) | copy-start | bytes 17668
  819.1 14.8 %copy-start.50 = (f32[512]{0:T(512)S(1)}, f32[512]{0:T(512)}, u32[]{:S(2)}) copy-start(f32[512]{0:T(512)} %copy-done.48) | copy-start | bytes 6148
  819.1 14.8 %copy-start.54 = (bf16[512,1152]{0,1:T(8,128)(2,1)S(1)}, bf16[512,1152]{0,1:T(8,128)(2,1)}, u32[]{:S(2)}) copy-start(bf16[512,1152]{0,1:T(8,128)(2,1)} %copy-done.53) | copy-start | bytes 3538948
  833.8 56.5 %copy-start.42 = (f32[512]{0:T(512)S(1)}, f32[512]{0:T(512)}, u32[]{:S(2)}) copy-start(f32[512]{0:T(512)} %copy-done.41) | copy-start | bytes 6148
  833.9 56.6 %copy-start.15 = (f32[512,1472]{0,1:T(8,128)S(1)}, f32[512,1472]{0,1:T(8,128)}, u32[]{:S(2)}) copy-start(f32[512,1472]{0,1:T(8,128)} %copy-done.14) | copy-start | bytes 9043972
  890.4 531.2 %copy-start.1 = (s32[2047]{0:T(1024)S(1)}, s32[2047]{0:T(1024)}, u32[]{:S(2)}) copy-start(s32[2047]{0:T(1024)} %param.15) | copy-start | bytes 24568
  (52 other events, 287.9 us)
Sparse Core Ops, SparseCore 0:
  10.9 66.2 all-gather.4
  80.2 87.6 all-gather.8
  170.8 87.3 all-gather.6
  261.0 96.6 all-gather.10
  582.9 143.2 reduce-scatter.12
  734.1 223.8 reduce-scatter.10
  966.2 223.5 reduce-scatter.8
  1197.9 223.5 reduce-scatter.6
where the time goes:
time: 1440 us; the launch traced here: 1430 us
  waiting for transfers between devices  583 us (40%)
  local copies, waits for them, and re-layouts  375 us (26%)
  matrix products  241 us (17%)
  starting transfers between devices  84.2 us (6%)
  other arithmetic  79.4 us (6%)
  blocking collectives  50 us (3%)
  between operations  16.2 us (1%)
    reduce_scatter x1, waiting for transfers between devices, shards(): lax.psum_scatter(d_w_gate, 'seq', scatter_dimension=1, tiled=True)  232 us
    reduce_scatter x1, waiting for transfers between devices, shards(): lax.psum_scatter(d_w_up, 'seq', scatter_dimension=1, tiled=True)  232 us
    dot_general x17, matrix products, matmul_nt(): lax.dot_general(left, right, (((1,), (1,)), ((), ())), preferred_element_...  102 us
    ppermute x24, starting transfers between devices, shifted(): return lax.ppermute(x, axis, pairs)  83.7 us
    another operation x12, local copies, waits for them, and re-layouts, toeplitz(): jnp.tile(line, row_count)[:row_count * (span_len - 1)]  73.6 us
    dot_general x17, matrix products, matmul(): return jnp.dot(left, right, preferred_element_type=jnp.float32)  70.9 us
    dot_general x17, matrix products, matmul_tn(): lax.dot_general(left, right, (((0,), (0,)), ((), ())), preferred_element_...  67.2 us
    reduce_scatter x1, waiting for transfers between devices, shards(): lax.psum_scatter(d_down, 'seq', scatter_dimension=0, tiled=True)  62.2 us
  transfers between devices with their start and end apart: 32, of which 7 were waited for; matrix products, arithmetic and copies ran while one was open for 40% of the time, Pallas kernels for 0%

commit v1 on v0

--- a/solution.py
+++ b/solution.py
@@ -1,7 +1,1141 @@
+import functools
+import math
 import jax
 import jax.numpy as jnp
 from jax import lax
+from jax.experimental import pallas as pl
+from jax.experimental.pallas import tpu as pltpu
 from jax.sharding import PartitionSpec as P
+
+MESH = pl.DeviceIdType.MESH
+BF = jnp.bfloat16
+F32 = jnp.float32
+BIG = 1e30
+GRIDS = {32: (4, 2, 2)}
+ORDERS = ("xyz", "zxy", "zyx")
+GROUPS = 8
+STAGES = 5
+PIECE = 48
+EPS = 1e-06
+
+
+def nt(a, b):
+    return lax.dot_general(a, b, (((1,), (1,)), ((), ())), preferred_element_type=F32)
+
+
+def nn(a, b):
+    return jnp.dot(a, b, preferred_element_type=F32)
+
+
+def column_parts(width):
+    return ((0, 256), (256, 640), (896, width - 896))
+
+
+def when(cond, body):
+    if cond is None:
+        body()
+    else:
+        pl.when(cond)(body)
+
+
+def inside(value, count):
+    return (value >= 0) & (value < count)
+
+
+class Place:
+    def __init__(self, n):
+        self.n = n
+        self.grid = GRIDS[n]
+        zs, ys, xs = self.grid
+        self.me = lax.axis_index("seq")
+        self.c = self.me % 2
+        chip = self.me // 2
+        self.x = chip % xs
+        self.y = (chip // xs) % ys
+        self.z = chip // (xs * ys)
+
+    def dev(self, z, y, x):
+        _, ys, xs = self.grid
+        return ((z * ys + y) * xs + x) * 2 + self.c
+
+    def around(self):
+        zs = self.grid[0]
+        z, y, x = self.z, self.y, self.x
+        out = [
+            (None, self.me + 1 - 2 * self.c),
+            (None, self.dev(z, y, 1 - x)),
+            (None, self.dev(z, 1 - y, x)),
+            (z < zs - 1, self.dev(jnp.minimum(z + 1, zs - 1), y, x)),
+            (z > 0, self.dev(jnp.maximum(z - 1, 0), y, x)),
+        ]
+        return out
+
+    def barrier(self, reach, far=False):
+        sem = pltpu.get_barrier_semaphore()
+        pairs = self.around()
+        if far:
+            zs = self.grid[0]
+            pairs = pairs[:3] + [(None, self.dev((self.z + i) % zs, self.y, self.x)) for i in range(1, zs)]
+        for by in reach:
+            target = self.me + by
+            pairs.append((inside(target, self.n), jnp.clip(target, 0, self.n - 1)))
+        count = 0
+        for cond, device in pairs:
+            when(
+                cond,
+                lambda device=device: pl.semaphore_signal(
+                    sem, inc=1, device_id=(device,), device_id_type=MESH
+                ),
+            )
+            count = count + (1 if cond is None else cond.astype(jnp.int32))
+        pl.semaphore_wait(sem, count)
+
+
+def gather_stages(here, blocks, send, recv, width):
+    zs, ys, xs = here.grid
+    z, y, x = here.z, here.y, here.x
+    parts = []
+    slot = 0
+    for order, (first, wide) in zip(ORDERS, column_parts(width)):
+        cols = pl.ds(first, wide)
+        have = set()
+        stages = []
+        for dim in order:
+            in_y = pl.ds(0, ys) if "y" in have else pl.ds(y, 1)
+            in_x = pl.ds(0, xs) if "x" in have else pl.ds(x, 1)
+            if dim == "z":
+                for step in range(zs - 1):
+                    moves = []
+                    for way in (1, -1):
+                        source = z - way * step
+                        sends = inside(source, zs) & inside(z + way, zs)
+                        gets = inside(z - way - way * step, zs) & inside(z - way, zs)
+                        in_z = pl.ds(jnp.clip(source, 0, zs - 1), 1)
+                        device = here.dev(jnp.clip(z + way, 0, zs - 1), y, x)
+                        moves.append((sends, gets, in_z, in_y, in_x, cols, device, slot))
+                        slot += 1
+                    stages.append(moves)
+            else:
+                in_z = pl.ds(0, zs) if "z" in have else pl.ds(z, 1)
+                device = here.dev(z, y, 1 - x) if dim == "x" else here.dev(z, 1 - y, x)
+                stages.append([(None, None, in_z, in_y, in_x, cols, device, slot)])
+                slot += 1
+            have.add(dim)
+        parts.append(stages)
+
+    def copy(move, g):
+        _, _, in_z, in_y, in_x, cols, device, at = move
+        ref = blocks.at[g, in_z, in_y, in_x, :, cols]
+        return pltpu.make_async_remote_copy(
+            ref, ref, send.at[g, at], recv.at[g, at], device_id=(device,), device_id_type=MESH
+        )
+
+    return parts, copy, slot
+
+
+def gather_round(parts, copy, r, ready):
+    for k in range(STAGES, -1, -1):
+        g = r - k
+
+        def step(g=g, k=k):
+            if k == 0:
+                ready(g)
+            for stages in parts:
+                if k > 0:
+                    for move in stages[k - 1]:
+                        when(move[1], lambda move=move: copy(move, g).wait_recv())
+                if k < STAGES:
+                    for move in stages[k]:
+                        when(move[0], lambda move=move: copy(move, g).start())
+
+        if isinstance(r, int):
+            if 0 <= g < GROUPS:
+                step()
+        else:
+            pl.when(inside(g, GROUPS))(step)
+
+
+def gather_drain(parts, copy):
+    def body(g, _):
+        for stages in parts:
+            for moves in stages:
+                for move in moves:
+                    when(move[0], lambda move=move: copy(move, g).wait_send())
+        return 0
+
+    lax.fori_loop(0, GROUPS, body, 0)
+
+
+def shift_line(table, rel, head):
+    line = jnp.zeros(table.shape, F32)
+    for bucket in range(rel.shape[0]):
+        line = jnp.where(table == bucket, rel[bucket, head], line)
+    return line
+
+
+def gelu_parts(v):
+    root = math.sqrt(2.0 / math.pi)
+    sq = v * v
+    t = jnp.tanh(root * (v + 0.044715 * (sq * v)))
+    half = 0.5 * (1.0 + t)
+    value = v * half
+    slope = half + 0.5 * v * (1.0 - t * t) * (root * (1.0 + 3 * 0.044715 * sq))
+    return value, slope
+
+
+def row_norm(v):
+    return lax.rsqrt(jnp.mean(v * v, axis=-1, keepdims=True) + EPS)
+
+
+REACH = (1, -1, 2, -2)
+
+
+def forward_kernel(
+    n, heads,
+    slab, hid, dy, kx_own, qx, table, rel, na, nf,
+    o_grads, o_outp, o_dn2p, o_x1, o_at, o_q, o_kv, o_kx, o_lse, o_ga,
+    G, ga, n2f, dyf, kv, kx, qv, x1, at, lse,
+    gs, gr, lsem, hs, hr, ks, kr, cs, cr, osem, stsem,
+):
+    here = Place(n)
+    c = here.c
+    rows, D = hid.shape
+    inner = qv.shape[1]
+    nz = here.grid[0]
+    partner = here.me + 1 - 2 * c
+    window = kv.shape[0]
+    tiles = rows // 256
+    span = (window - rows) + 256
+    mine = pl.ds(pl.multiple_of(c * rows, rows), rows)
+    centre = pl.ds(2 * rows, rows)
+
+    def to_partner(src, dst, i):
+        return pltpu.make_async_remote_copy(
+            src, dst, cs.at[i], cr.at[i], device_id=(partner,), device_id_type=MESH
+        )
+
+    def halo(ref, by, i, send, recv):
+        return pltpu.make_async_remote_copy(
+            ref.at[centre],
+            ref.at[pl.ds((2 - by) * rows, rows)],
+            send.at[i],
+            recv.at[i],
+            device_id=(jnp.clip(here.me + by, 0, n - 1),),
+            device_id_type=MESH,
+        )
+
+    def halo_each(ref, send, recv, what):
+        for i, by in enumerate(REACH):
+            to, frm = inside(here.me + by, n), inside(here.me - by, n)
+            if what == "start":
+                when(to, lambda i=i, by=by: halo(ref, by, i, send, recv).start())
+            elif what == "recv":
+                when(frm, lambda i=i, by=by: halo(ref, by, i, send, recv).wait_recv())
+            else:
+                when(to, lambda i=i, by=by: halo(ref, by, i, send, recv).wait_send())
+
+    own = [
+        pltpu.make_async_copy(slab.at[g], G.at[g, here.z, here.y, here.x], lsem.at[g])
+        for g in range(GROUPS)
+    ]
+    for copy in own:
+        copy.start()
+    kx_in = pltpu.make_async_copy(kx_own, kx.at[centre], lsem.at[GROUPS])
+    kx_in.start()
+    dy_in = pltpu.make_async_copy(dy, dyf.at[mine], lsem.at[GROUPS + 1])
+    dy_in.start()
+    here.barrier(REACH)
+    for copy in own:
+        copy.wait()
+    parts, copy, _ = gather_stages(here, G, gs, gr, D)
+    ag = lambda r: gather_round(parts, copy, r, lambda g: None)
+    ag(0)
+    kx_in.wait()
+    halo_each(kx, ks, kr, "start")
+    dy_in.wait()
+    dy_out = to_partner(dyf.at[mine], dyf.at[mine], 0)
+    dy_out.start()
+    edge = jnp.where(lax.broadcasted_iota(jnp.int32, (rows, 128), 1) == 25, -BIG, 0.0).astype(BF)
+    for by in REACH:
+        def absent(by=by):
+            at_rows = pl.ds((2 - by) * rows, rows)
+            kv[at_rows, :] = jnp.zeros((rows, kv.shape[1]), BF)
+            kx[at_rows, :] = edge
+        pl.when(jnp.logical_not(inside(here.me - by, n)))(absent)
+
+    def attention(n1, bias, vt, S, Pm):
+        ag(1)
+
+        def norm_rows(i, _):
+            at_rows = pl.ds(i * 64, 64)
+            v = hid[at_rows, :].astype(F32)
+            n1[at_rows, :] = (v * row_norm(v) * na[...]).astype(BF)
+            return 0
+
+        lax.fori_loop(0, rows // 64, norm_rows, 0)
+        ag(2)
+        lines = table.shape[0]
+        for head in range(heads):
+            line = shift_line(table[...], rel, head)
+            for b in range(bias.shape[1] // 128):
+                lo = line[19 - b : 20 - b, :]
+                hi = line[18 - b : 19 - b, :]
+                both = jnp.broadcast_to(jnp.concatenate([lo, hi], 1), (128, 256))
+                bias[head, 128 * b : 128 * b + 128, :] = pltpu.roll(both, 0, 1, stride=1, stride_axis=0)[:, :128]
+            if head == 1:
+                ag(3)
+            if head == 3:
+                ag(4)
+        ag(5)
+        keep = pltpu.make_async_copy(G.at[0], ga.at[:, :, :, c], lsem.at[GROUPS + 2])
+        keep.start()
+        give = to_partner(G.at[0], ga.at[:, :, :, c], 1)
+        give.start()
+        keep.wait()
+        give.wait_recv()
+        ga_out = pltpu.make_async_copy(ga, o_ga, osem.at[1])
+        ga_out.start()
+
+        for part in (1, 2, 0):
+            weight = ga[part].reshape(inner, D)
+            for half in range(rows // 256):
+                at_rows = pl.ds(256 * half, 256)
+                got = nt(n1[at_rows, :], weight).astype(BF)
+                if part == 0:
+                    qv[at_rows, :] = got
+                else:
+                    kv[pl.ds(2 * rows + 256 * half, 256), (part - 1) * inner : part * inner] = got
+        halo_each(kv, hs, hr, "start")
+        ag(6)
+        halo_each(kx, ks, kr, "recv")
+        halo_each(kv, hs, hr, "recv")
+        kv_out = pltpu.make_async_copy(kv, o_kv, osem.at[2])
+        kv_out.start()
+        kx_out = pltpu.make_async_copy(kx, o_kx, osem.at[3])
+        kx_out.start()
+        q_out = pltpu.make_async_copy(qv, o_q, osem.at[4])
+        q_out.start()
+
+        def turn(i, _):
+            at_rows = pl.ds(pl.multiple_of(i * 256, 256), 256)
+            vt[:, at_rows] = kv[at_rows, inner:].T
+            return 0
+
+        lax.fori_loop(0, window // 256, turn, 0)
+        lane = lax.broadcasted_iota(jnp.int32, (256, 128), 1) // 64
+
+        def pair(hp, _):
+            @pl.when(hp > 0)
+            def _():
+                ag(hp + 6)
+
+            cols = pl.ds(pl.multiple_of(hp * 128, 128), 128)
+
+            def one(k, _):
+                t, e = k // 2, k % 2
+                base = pl.multiple_of(t * 256, 256)
+                head = hp * 2 + e
+                q = qv[pl.ds(base, 256), cols]
+                q = jnp.where(lane == e, q, jnp.zeros_like(q))
+                qa = jnp.concatenate([q, qx[pl.ds(base, 256), :]], 1)
+
+                def score(b, m):
+                    at_rows = pl.ds(pl.multiple_of(base + b * 256, 256), 256)
+                    ka = jnp.concatenate([kv[at_rows, cols], kx[at_rows, :]], 1)
+                    s = nt(ka, qa)
+                    low = pl.multiple_of(b * 256, 256)
+                    plane = jnp.concatenate(
+                        [bias[head, pl.ds(low + 128, 256), :], bias[head, pl.ds(low, 256), :]], 1
+                    )
+                    s = s + plane
+                    S[pl.ds(low, 256), :] = s
+                    return jnp.maximum(m, jnp.max(s.reshape(32, 8, 256), axis=0))
+
+                m = lax.fori_loop(0, span // 256, score, jnp.full((8, 256), -3e38, F32))
+                m = jnp.max(m, axis=0, keepdims=True)
+
+                def weigh(b, total):
+                    at_rows = pl.ds(pl.multiple_of(b * 256, 256), 256)
+                    p = jnp.exp(S[at_rows, :] - m)
+                    Pm[at_rows, :] = p.astype(BF)
+                    return total + jnp.sum(p.reshape(32, 8, 256), axis=0)
+
+                total = lax.fori_loop(0, span // 256, weigh, jnp.zeros((8, 256), F32))
+                total = jnp.sum(total, axis=0, keepdims=True)
+                out_rows = pl.ds(pl.multiple_of(head * 64, 64), 64)
+                mixed = nn(vt[out_rows, pl.ds(base, span)], Pm[...])
+                at[out_rows, pl.ds(base, 256)] = mixed / total
+                lse[pl.ds(head, 1), pl.ds(base, 256)] = m + jnp.log(total)
+                return 0
+
+            lax.fori_loop(0, 2 * tiles, one, 0)
+            return 0
+
+        lax.fori_loop(0, heads // 2, pair, 0)
+        outs = [
+            pltpu.make_async_copy(at, o_at, osem.at[5]),
+            pltpu.make_async_copy(lse, o_lse, osem.at[6]),
+        ]
+        for o in outs:
+            o.start()
+        w_out = ga[3].reshape(inner, D)
+
+        def after(i, _):
+            at_rows = pl.ds(pl.multiple_of(i * 128, 128), 128)
+            a = at[:, at_rows].T.astype(BF)
+            v = hid[at_rows, :].astype(F32) + nn(a, w_out)
+            x1[at_rows, :] = v
+            n2f[pl.ds(pl.multiple_of(c * rows + i * 128, 128), 128), :] = (v * row_norm(v) * nf[...]).astype(BF)
+            return 0
+
+        lax.fori_loop(0, rows // 128, after, 0)
+        n2_out = to_partner(n2f.at[mine], n2f.at[mine], 2)
+        n2_out.start()
+        x1_out = pltpu.make_async_copy(x1, o_x1, osem.at[7])
+        x1_out.start()
+        give.wait_send()
+        n2_out.wait()
+        dy_out.wait()
+        halo_each(kx, ks, kr, "send")
+        halo_each(kv, hs, hr, "send")
+        for o in outs + [ga_out, kv_out, kx_out, q_out, x1_out]:
+            o.wait()
+
+    pl.run_scoped(
+        attention,
+        pltpu.VMEM((rows, D), BF),
+        pltpu.VMEM((heads, span + 128, 128), F32),
+        pltpu.VMEM((inner, window), BF),
+        pltpu.VMEM((span, 256), F32),
+        pltpu.VMEM((span, 256), BF),
+    )
+
+    def feed(acc_o, acc_n, ft, gt, ut, stage):
+        acc_o[...] = jnp.zeros_like(acc_o)
+        acc_n[...] = jnp.zeros_like(acc_n)
+
+        def stage_out(j):
+            return pltpu.make_async_copy(stage.at[j % 2], o_grads.at[j + 1], stsem.at[j % 2])
+
+        def chunk(j, _):
+            ag(j + 9)
+            g = j + 1
+            wg = G.at[g, :, :, :, pl.ds(0, 16), :]
+            wu = G.at[g, :, :, :, pl.ds(16, 16), :]
+            wd = G.at[g, :, :, :, pl.ds(32, 16), :]
+            whole = lambda ref: ref[...].reshape(256, D)
+
+            def tokens(i, _):
+                at_rows = pl.ds(pl.multiple_of(i * 256, 256), 256)
+                n2 = n2f[at_rows, :]
+                gate = nt(whole(wg), n2)
+                up = nt(whole(wu), n2)
+                df = nt(whole(wd), dyf[at_rows, :])
+                value, slope = gelu_parts(gate)
+                f = (value * up).astype(BF)
+                dg = (df * up * slope).astype(BF)
+                du = (df * value).astype(BF)
+                ft[:, at_rows] = f
+                gt[:, at_rows] = dg
+                ut[:, at_rows] = du
+                acc_o[at_rows, :] += nn(f.T, whole(wd))
+                acc_n[at_rows, :] += nn(dg.T, whole(wg)) + nn(du.T, whole(wu))
+                return 0
+
+            lax.fori_loop(0, 2 * rows // 256, tokens, 0)
+
+            @pl.when(j >= 2)
+            def _():
+                stage_out(j - 2).wait()
+
+            s = j % 2
+            stage[s, :, :, :, 0:16, :] = nn(gt[...], n2f[...]).astype(BF).reshape(here.grid + (16, D))
+            stage[s, :, :, :, 16:32, :] = nn(ut[...], n2f[...]).astype(BF).reshape(here.grid + (16, D))
+            stage[s, :, :, :, 32:48, :] = nn(ft[...], dyf[...]).astype(BF).reshape(here.grid + (16, D))
+            stage_out(j).start()
+            return 0
+
+        lax.fori_loop(0, GROUPS - 1, chunk, 0)
+        outs = [
+            pltpu.make_async_copy(acc_o, o_outp, osem.at[0]),
+            pltpu.make_async_copy(acc_n, o_dn2p, osem.at[1]),
+        ]
+        for o in outs:
+            o.start()
+        gather_drain(parts, copy)
+        for o in outs:
+            o.wait()
+        stage_out(GROUPS - 3).wait()
+        stage_out(GROUPS - 2).wait()
+
+    pl.run_scoped(
+        feed,
+        pltpu.VMEM((2 * rows, D), F32),
+        pltpu.VMEM((2 * rows, D), F32),
+        pltpu.VMEM((256, 2 * rows), BF),
+        pltpu.VMEM((256, 2 * rows), BF),
+        pltpu.VMEM((256, 2 * rows), BF),
+        pltpu.VMEM((2,) + here.grid + (PIECE, D), BF),
+    )
+
+
+def forward_call(n, heads, slab, hid, dy, kx_own, qx, table, rel, na, nf):
+    rows, D = hid.shape
+    inner = heads * 64
+    zs, ys, xs = GRIDS[n]
+    window = 5 * rows
+    span = window - rows + 256
+    shape = jax.ShapeDtypeStruct
+    any_, vm = pl.BlockSpec(memory_space=pl.ANY), pl.BlockSpec(memory_space=pltpu.VMEM)
+    sm = pl.BlockSpec(memory_space=pltpu.SMEM)
+    slots = 3 * 8
+    dma = pltpu.SemaphoreType.DMA
+    return pl.pallas_call(
+        functools.partial(forward_kernel, n, heads),
+        out_shape=(
+            shape((GROUPS, zs, ys, xs, PIECE, D), BF),
+            shape((2 * rows, D), F32),
+            shape((2 * rows, D), F32),
+            shape((rows, D), F32),
+            shape((inner, rows), F32),
+            shape((rows, inner), BF),
+            shape((window, 2 * inner), BF),
+            shape((window, 128), BF),
+            shape((8, rows), F32),
+            shape((zs, ys, xs, 2, PIECE, D), BF),
+        ),
+        in_specs=[any_, vm, any_, any_, vm, vm, sm, vm, vm],
+        out_specs=(any_,) * 10,
+        scratch_shapes=[
+            pltpu.VMEM((GROUPS, zs, ys, xs, PIECE, D), BF),
+            pltpu.VMEM((zs, ys, xs, 2, PIECE, D), BF),
+            pltpu.VMEM((2 * rows, D), BF),
+            pltpu.VMEM((2 * rows, D), BF),
+            pltpu.VMEM((window, 2 * inner), BF),
+            pltpu.VMEM((window, 128), BF),
+            pltpu.VMEM((rows, inner), BF),
+            pltpu.VMEM((rows, D), F32),
+            pltpu.VMEM((inner, rows), F32),
+            pltpu.VMEM((8, rows), F32),
+            dma((GROUPS, slots)), dma((GROUPS, slots)),
+            dma((GROUPS + 3,)),
+            dma((4,)), dma((4,)), dma((4,)), dma((4,)),
+            dma((3,)), dma((3,)),
+            dma((8,)), dma((2,)),
+        ],
+        compiler_params=pltpu.CompilerParams(
+            collective_id=1, has_side_effects=True, vmem_limit_bytes=63 * 2**20
+        ),
+        cost_estimate=pl.CostEstimate(flops=55 * 10**9, bytes_accessed=80 * 10**6, transcendentals=10**7),
+        name="forward",
+    )(slab, hid, dy, kx_own, qx, table, rel, na, nf)
+
+
+def prepare(hidden, segments, delete_mask, bucket_table, attn_weight, gate_weight, up_weight, down_weight):
+    D = hidden.shape[1]
+    rows = hidden.shape[0]
+    groups = GROUPS - 1
+    ffn = jnp.stack([gate_weight.T, up_weight.T, down_weight]).reshape(3, groups, 16, D)
+    ffn = jnp.transpose(ffn, (1, 0, 2, 3)).reshape(groups, PIECE, D)
+    slab = jnp.concatenate([attn_weight.T[None], ffn], 0)
+    lane = jnp.arange(128, dtype=jnp.int32)[None, :]
+    seg = segments[:, None]
+    digit = jnp.where(lane < 9, seg % 8, jnp.where(lane < 17, (seg // 8) % 8, seg // 64))
+    hit = digit == (lane - 1) % 8
+    coded = (lane >= 1) & (lane < 25)
+    kx = jnp.where(lane == 0, delete_mask.astype(F32)[:, None], jnp.where(coded & ~hit, -BIG, 0.0)).astype(BF)
+    qx = jnp.where((lane == 0) | (lane == 25) | (coded & hit), 1.0, 0.0).astype(BF)
+    reach = bucket_table.shape[0]
+    table = jnp.pad(jnp.flip(bucket_table), (257, 20 * 128 - 257 - reach), constant_values=-1).reshape(20, 128)
+    table = jnp.pad(table, ((0, 4), (0, 0)), constant_values=-1)
+    return slab, kx, qx, table
+
+
+FIRST = (1, 2, 3, 4, 5, 0, 6, 7)
+AT = 5
+SLOTS = 3
+WORK = 6
+LINES = 56
+
+
+def group_of(pos):
+    if isinstance(pos, int):
+        return FIRST[pos]
+    return jnp.where(pos < AT, pos + 1, jnp.where(pos == AT, 0, pos))
+
+
+def add_into(dst, src):
+    dst[...] = (dst[...].astype(F32) + src[...].astype(F32)).astype(BF)
+
+
+class Scatter:
+    def __init__(self, here, source, work, land, landa, landz, result, send, recv, load, width):
+        self.here, self.source, self.work, self.result = here, source, work, result
+        self.land, self.landa, self.landz = land, landa, landz
+        self.send, self.recv, self.load = send, recv, load
+        self.parts = column_parts(width)
+
+    def loading(self, part, pos):
+        here = self.here
+        zs, ys, xs = here.grid
+        in_y = pl.ds(here.y, 1) if part == 1 else pl.ds(0, ys)
+        in_x = pl.ds(here.x, 1) if part == 2 else pl.ds(0, xs)
+        cols = pl.ds(*self.parts[part])
+        return pltpu.make_async_copy(
+            self.source.at[group_of(pos), :, in_y, in_x, :, cols],
+            self.work.at[pos % WORK, :, in_y, in_x, :, cols],
+            self.load.at[pos, part],
+        )
+
+    def start_load(self, pos):
+        for part in range(3):
+            self.loading(part, pos).start()
+
+    def moves(self, part, k, pos):
+        here = self.here
+        zs, ys, xs = here.grid
+        z, y, x = here.z, here.y, here.x
+        cols = pl.ds(*self.parts[part])
+        dim = (("z0", "z1", "z2", "y", "x"), ("y", "x", "z0", "z1", "z2"), ("x", "y", "z0", "z1", "z2"))[part][k]
+        work, source, g = self.work, self.source, group_of(pos)
+        w, slot = pos % WORK, pos % SLOTS
+        base = 8 * part
+
+        def remote(src, dst, at, device):
+            return pltpu.make_async_remote_copy(
+                src, dst, self.send.at[pos, at], self.recv.at[pos, at], device_id=(device,), device_id_type=MESH
+            )
+
+        if dim[0] == "z":
+            step = int(dim[1])
+            out = []
+            for turn, way in enumerate((1, -1)):
+                target = z + way * (zs - 1 - step)
+                got = z + way * (zs - 2 - step)
+                sends = inside(z + way, zs) & inside(target, zs)
+                gets = inside(z - way, zs) & inside(got, zs)
+                spot = step if turn == 0 or step == 0 else step + 2
+                device = here.dev(jnp.clip(z + way, 0, zs - 1), y, x)
+                block, mine = jnp.clip(target, 0, zs - 1), jnp.clip(got, 0, zs - 1)
+                if part == 0:
+                    src, dst = work.at[w, block, :, :, :, cols], self.landa.at[slot, spot]
+                else:
+                    src, dst = work.at[w, block, y, x, :, cols], self.landz.at[slot, spot, :, cols]
+
+                def consume(mine=mine, dst=dst):
+                    if part == 0:
+                        for b in range(ys):
+                            add_into(work.at[w, mine, b, :, :, cols], dst.at[b])
+                    elif step < zs - 2:
+                        add_into(work.at[w, mine, y, x, :, cols], dst)
+
+                out.append((sends, gets, remote(src, dst, base + 2 + 2 * step + turn, device), consume))
+            return out
+        at = base + (0 if dim == "y" else 1)
+        device = here.dev(z, 1 - y, x) if dim == "y" else here.dev(z, y, 1 - x)
+        if k == 0 and dim == "y":
+            src = source.at[g, :, pl.ds(1 - y, 1), :, :, cols]
+            dst = work.at[w, :, pl.ds(y, 1), :, :, cols]
+            pairs = [(work.at[w, b, y, :, :, cols], work.at[w, b, 1 - y, :, :, cols]) for b in range(zs)]
+        elif k == 0:
+            src = source.at[g, :, :, pl.ds(1 - x, 1), :, cols]
+            dst = work.at[w, :, :, pl.ds(x, 1), :, cols]
+            pairs = [(work.at[w, b, :, x, :, cols], work.at[w, b, :, 1 - x, :, cols]) for b in range(zs)]
+        elif part != 0:
+            src = work.at[w, :, y, 1 - x, :, cols] if dim == "x" else work.at[w, :, 1 - y, x, :, cols]
+            dst = self.land.at[slot, :, :, cols]
+            pairs = [(work.at[w, b, y, x, :, cols], self.land.at[slot, b, :, cols]) for b in range(zs)]
+        elif dim == "y":
+            src = work.at[w, z, 1 - y, :, :, cols]
+            dst = self.land.at[slot, pl.ds(0, xs), :, cols]
+            pairs = [(work.at[w, z, y, b, :, cols], self.land.at[slot, b, :, cols]) for b in range(xs)]
+        else:
+            src = work.at[w, z, y, 1 - x, :, cols]
+            dst = self.land.at[slot, xs, :, cols]
+            pairs = []
+
+        def consume():
+            for to, frm in pairs:
+                add_into(to, frm)
+
+        return [(None, None, remote(src, dst, at, device), consume)]
+
+    def finish(self, part, pos):
+        here = self.here
+        zs, ys, xs = here.grid
+        z, y, x = here.z, here.y, here.x
+        slot, g = pos % SLOTS, group_of(pos)
+        first, wide = self.parts[part]
+        cols = pl.ds(first, wide)
+        own = self.work[pos % WORK, z, y, x, :, cols].astype(F32)
+        if part == 0:
+            self.result[g, :, cols] = own + self.land[slot, xs, :, cols].astype(F32)
+            return
+        up = self.landz[slot, zs - 2, :, cols].astype(F32)
+        down = self.landz[slot, zs, :, cols].astype(F32)
+        self.result[g, :, cols] = own + jnp.where(z > 0, up, 0.0) + jnp.where(z < zs - 1, down, 0.0)
+
+    def round(self, r):
+        for k in range(STAGES, -1, -1):
+            pos = r - k
+
+            def step(pos=pos, k=k):
+                for part in range(3):
+                    if k == (0 if part == 0 else 1):
+                        self.loading(part, pos).wait()
+                    if k > 0:
+                        for _, gets, copy, consume in self.moves(part, k - 1, pos):
+                            def take(copy=copy, consume=consume):
+                                copy.wait_recv()
+                                consume()
+
+                            when(gets, take)
+                    if k < STAGES:
+                        for sends, _, copy, _ in self.moves(part, k, pos):
+                            when(sends, lambda copy=copy: copy.start())
+                        continue
+                    self.finish(part, pos)
+                    for stage in range(STAGES):
+                        for sends, _, copy, _ in self.moves(part, stage, pos):
+                            when(sends, lambda copy=copy: copy.wait_send())
+                if k == STAGES:
+                    when(pos + WORK < GROUPS, lambda: self.start_load(pos + WORK))
+
+            if isinstance(pos, int):
+                if 0 <= pos < GROUPS:
+                    step()
+            else:
+                pl.when(inside(pos, GROUPS))(step)
+
+
+def norm_back(v, gain, d):
+    r = row_norm(v)
+    vr = v * r
+    dg = d * gain
+    return r * (dg - vr * jnp.mean(vr * dg, axis=-1, keepdims=True)), d * vr
+
+
+def put_line(small, first, line):
+    width = line.shape[1]
+    for i in range(-(-width // 128)):
+        wide = min(128, width - 128 * i)
+        small[first + i : first + i + 1, 0:wide] = line[:, 128 * i : 128 * i + wide]
+
+
+def backward_kernel(
+    n, heads,
+    grads, outp, dn2p, x1_in, at_in, q_in, kv_in, kx_in, lse, ga_in,
+    hid, dy, qx, table, rel, na, nf,
+    gr, o_out, o_dh, o_res, o_small, dn_land, op_land,
+    work, land, landa, landz, res, dx1, kv, kx, qv, at, ga, dat, das, back, fold, small, sland,
+    ss, rs, lds, cs, cr, hs, hr, ls, ps, pr, osem,
+):
+    here = Place(n)
+    c = here.c
+    rows, D = dx1.shape
+    inner = qv.shape[1]
+    window = kv.shape[0]
+    zs, ys, xs = here.grid
+    z, y, x = here.z, here.y, here.x
+    span = window - rows + 256
+    partner = here.me + 1 - 2 * c
+    mine = pl.ds(pl.multiple_of(c * rows, rows), rows)
+    theirs = pl.ds(pl.multiple_of((1 - c) * rows, rows), rows)
+
+    def to_partner(src, dst, i):
+        return pltpu.make_async_remote_copy(
+            src, dst, cs.at[i], cr.at[i], device_id=(partner,), device_id_type=MESH
+        )
+
+    def local(src, dst, i):
+        return pltpu.make_async_copy(src, dst, ls.at[i])
+
+    sc = Scatter(here, gr, work, land, landa, landz, res, ss, rs, lds, D)
+    for pos in range(WORK):
+        if pos != AT:
+            sc.start_load(pos)
+    loads = [
+        local(dn2p.at[mine], dx1, 0), local(kv_in, kv, 1), local(kx_in, kx, 2),
+        local(q_in, qv, 3), local(at_in, at, 4), local(ga_in, ga, 5),
+    ]
+    for load in loads:
+        load.start()
+    here.barrier(REACH, True)
+    dn_out = to_partner(dn2p.at[theirs], dn_land, 0)
+    dn_out.start()
+    sc.round(0)
+    op_out = to_partner(outp.at[theirs], op_land, 1)
+    op_out.start()
+    small[...] = jnp.zeros_like(small)
+
+    def after_ffn(x1, other, grad, low):
+        first = [local(x1_in, x1, 6), local(dy, grad, 7)]
+        for load in first:
+            load.start()
+        dn_out.wait_recv()
+        second = local(dn_land, other, 8)
+        second.start()
+        for load in loads + first + [second]:
+            load.wait()
+        w_out = ga[zs - 1].reshape(inner, D)
+
+        def through(i, total):
+            at_rows = pl.ds(pl.multiple_of(i * 128, 128), 128)
+            d = dx1[at_rows, :] + other[at_rows, :]
+            back_v, gain_d = norm_back(x1[at_rows, :], nf[...], d)
+            v = grad[at_rows, :].astype(F32) + back_v
+            dx1[at_rows, :] = v
+            v = v.astype(BF)
+            low[at_rows, :] = v
+            da = nt(v, w_out).astype(BF)
+            das[at_rows, :] = da
+            dat[:, at_rows] = da.T
+            return total + jnp.sum(gain_d.reshape(16, 8, D), axis=0)
+
+        total = lax.fori_loop(0, rows // 128, through, jnp.zeros((8, D), F32))
+        put_line(small, 44, jnp.sum(total, axis=0, keepdims=True))
+        third = local(outp.at[mine], other, 9)
+        third.start()
+        sc.round(1)
+        for h in range(2):
+            part = nn(at[pl.ds(h * (inner // 2), inner // 2), :].astype(BF), low[...])
+            ga[zs - 1, h] = part.astype(BF).reshape(xs, 2, PIECE, D)
+        third.wait()
+        op_out.wait_recv()
+
+        def add(i, _):
+            at_rows = pl.ds(pl.multiple_of(i * 64, 64), 64)
+            x1[at_rows, :] = x1[at_rows, :] + other[at_rows, :]
+            return 0
+
+        lax.fori_loop(0, rows // 64, add, 0)
+        fourth = local(op_land, other, 10)
+        fourth.start()
+        fourth.wait()
+
+        def put(i, _):
+            at_rows = pl.ds(pl.multiple_of(i * 64, 64), 64)
+            low[at_rows, :] = (x1[at_rows, :] + other[at_rows, :]).astype(BF)
+            return 0
+
+        lax.fori_loop(0, rows // 64, put, 0)
+        out = pltpu.make_async_copy(low, o_out, osem.at[0])
+        out.start()
+        out.wait()
+        dn_out.wait_send()
+        op_out.wait_send()
+
+    pl.run_scoped(
+        after_ffn, pltpu.VMEM((rows, D), F32), pltpu.VMEM((rows, D), F32), pltpu.VMEM((rows, D), BF),
+        pltpu.VMEM((rows, D), BF),
+    )
+
+    def home(dkv, hp, by, i):
+        return pltpu.make_async_remote_copy(
+            dkv.at[hp, pl.ds((2 + by) * rows, rows)],
+            back.at[hp, i],
+            hs.at[hp, i],
+            hr.at[hp, i],
+            device_id=(jnp.clip(here.me + by, 0, n - 1),),
+            device_id_type=MESH,
+        )
+
+    def attention(acc_k, acc_v, skew, kt, bias, dkv, dqt, n1, proj, proj_t, hid_v):
+        hid_in = local(hid, hid_v, 11)
+        hid_in.start()
+
+        def turn(i, _):
+            at_rows = pl.ds(pl.multiple_of(i * 256, 256), 256)
+            kt[:, at_rows] = kv[at_rows, 0:inner].T
+            return 0
+
+        lax.fori_loop(0, window // 256, turn, 0)
+        dqt[...] = jnp.zeros_like(dqt)
+        lane = lax.broadcasted_iota(jnp.int32, (256, 128), 1) // 64
+        lane_of = lax.broadcasted_iota(jnp.int32, (32, 128), 1)
+        blocks = skew.shape[0] // 128
+
+        def one_head(hp, e):
+            head = hp * 2 + e
+            cols = pl.ds(pl.multiple_of(hp * 128, 128), 128)
+            vcols = pl.ds(pl.multiple_of(inner + hp * 128, 128), 128)
+            out_rows = pl.ds(pl.multiple_of(head * 64, 64), 64)
+            line = shift_line(table[...], rel, head)
+            for b in range(blocks):
+                both = jnp.concatenate([line[19 - b : 20 - b, :], line[18 - b : 19 - b, :]], 1)
+                both = jnp.broadcast_to(both, (128, 256))
+                bias[128 * b : 128 * b + 128, :] = pltpu.roll(both, 0, 1, stride=1, stride_axis=0)[:, :128]
+            skew[...] = jnp.zeros_like(skew)
+
+            def tile(t, _):
+                base = pl.multiple_of(t * 256, 256)
+                here_q = pl.ds(base, 256)
+                q = qv[here_q, cols]
+                q = jnp.where(lane == e, q, jnp.zeros_like(q))
+                qa = jnp.concatenate([q, qx[here_q, :]], 1)
+                da = das[here_q, cols]
+                da = jnp.where(lane == e, da, jnp.zeros_like(da))
+                logs = lse[pl.ds(head, 1), here_q]
+                delta = jnp.sum(dat[out_rows, here_q].astype(F32) * at[out_rows, here_q], axis=0, keepdims=True)
+
+                def block(b, dq):
+                    low = pl.multiple_of(b * 256, 256)
+                    at_rows = pl.ds(pl.multiple_of(base + b * 256, 256), 256)
+                    ka = jnp.concatenate([kv[at_rows, cols], kx[at_rows, :]], 1)
+                    plane = jnp.concatenate([bias[pl.ds(low + 128, 256), :], bias[pl.ds(low, 256), :]], 1)
+                    p = jnp.exp(nt(ka, qa) + plane - logs)
+                    ds = p * (nt(kv[at_rows, vcols], da) - delta)
+                    skew[pl.ds(low + 128, 256), :] += ds[:, 0:128]
+                    skew[pl.ds(low, 256), :] += ds[:, 128:256]
+                    dsr = ds.astype(BF)
+                    acc_v[at_rows, :] += nn(p.astype(BF), da)
+                    acc_k[at_rows, :] += nn(dsr, q)
+                    return dq + nn(kt[out_rows, at_rows], dsr)
+
+                dqt[out_rows, here_q] = lax.fori_loop(0, span // 256, block, jnp.zeros((64, 256), F32))
+                return 0
+
+            lax.fori_loop(0, rows // 256, tile, 0)
+            tail = [None] * (blocks + 1)
+            for b in range(blocks):
+                a = jnp.concatenate([skew[128 * b : 128 * b + 128, :], jnp.zeros((128, 128), F32)], 1)
+                half = 64
+                while half >= 1:
+                    a = a[0:half] + pltpu.roll(a[half : 2 * half], 256 - half, 1)
+                    half //= 2
+                for at_line, part in ((19 - b, a[:, 0:128]), (18 - b, a[:, 128:256])):
+                    tail[at_line] = part if tail[at_line] is None else tail[at_line] + part
+            line_d = jnp.concatenate(tail + [jnp.zeros((4, 128), F32)], 0)
+            sums = [
+                jnp.sum(jnp.where(table[...] == b, line_d, 0.0), axis=0, keepdims=True) for b in range(rel.shape[0])
+            ]
+            sums = jnp.sum(jnp.concatenate(sums, 0), axis=1, keepdims=True)
+            small[0:32, :] = jnp.where(lane_of == head, sums, small[0:32, :])
+
+        def pair(hp, _):
+            sc.round(hp + 2)
+            acc_k[...] = jnp.zeros_like(acc_k)
+            acc_v[...] = jnp.zeros_like(acc_v)
+            lax.fori_loop(0, 2, lambda e, _: (one_head(hp, e), 0)[1], 0)
+
+            def pack(i, _):
+                at_rows = pl.ds(pl.multiple_of(i * 128, 128), 128)
+                dkv[hp, at_rows, 0:128] = acc_k[at_rows, :].astype(BF)
+                dkv[hp, at_rows, 128:256] = acc_v[at_rows, :].astype(BF)
+                return 0
+
+            lax.fori_loop(0, window // 128, pack, 0)
+            for i, by in enumerate(REACH):
+                when(inside(here.me + by, n), lambda i=i, by=by: home(dkv, hp, by, i).start())
+            return 0
+
+        lax.fori_loop(0, heads // 2, pair, 0)
+        hid_in.wait()
+
+        def norm_rows(i, _):
+            at_rows = pl.ds(pl.multiple_of(i * 64, 64), 64)
+            v = hid_v[at_rows, :].astype(F32)
+            n1[at_rows, :] = (v * row_norm(v) * na[...]).astype(BF)
+            return 0
+
+        lax.fori_loop(0, rows // 64, norm_rows, 0)
+
+        def gather_pair(hp, _):
+            for i, by in enumerate(REACH):
+                frm = inside(here.me - by, n)
+                when(frm, lambda i=i, by=by: home(dkv, hp, by, i).wait_recv())
+
+                def absent(i=i):
+                    back[hp, i] = jnp.zeros((rows, 256), BF)
+
+                when(jnp.logical_not(frm), absent)
+
+            def sum_rows(j, _):
+                at_rows = pl.ds(pl.multiple_of(j * 128, 128), 128)
+                total = dkv[hp, pl.ds(pl.multiple_of(2 * rows + j * 128, 128), 128), :].astype(F32)
+                for i in range(4):
+                    total = total + back[hp, i, at_rows, :].astype(F32)
+                total = total.astype(BF)
+                for part in range(2):
+                    piece = total[:, 128 * part : 128 * part + 128]
+                    to = pl.ds(pl.multiple_of((1 + part) * inner + hp * 128, 128), 128)
+                    proj[at_rows, to] = piece
+                    proj_t[to, at_rows] = piece.T
+                to = pl.ds(pl.multiple_of(hp * 128, 128), 128)
+                piece = dqt[to, at_rows].astype(BF)
+                proj_t[to, at_rows] = piece
+                proj[at_rows, to] = piece.T
+                return 0
+
+            lax.fori_loop(0, rows // 128, sum_rows, 0)
+            return 0
+
+        lax.fori_loop(0, heads // 2, gather_pair, 0)
+
+        def to_hidden(i, total):
+            at_rows = pl.ds(pl.multiple_of(i * 128, 128), 128)
+            d = nn(proj[at_rows, 0:inner], ga[0].reshape(inner, D))
+            d = d + nn(proj[at_rows, inner : 2 * inner], ga[1].reshape(inner, D))
+            d = d + nn(proj[at_rows, 2 * inner : 3 * inner], ga[2].reshape(inner, D))
+            back_v, gain_d = norm_back(hid_v[at_rows, :].astype(F32), na[...], d)
+            dx1[at_rows, :] = dx1[at_rows, :] + back_v
+            return total + jnp.sum(gain_d.reshape(16, 8, D), axis=0)
+
+        total = lax.fori_loop(0, rows // 128, to_hidden, jnp.zeros((8, D), F32))
+        put_line(small, 32, jnp.sum(total, axis=0, keepdims=True))
+        dh_out = pltpu.make_async_copy(dx1, o_dh, osem.at[1])
+        dh_out.start()
+
+        for part in range(3):
+            for h in range(2):
+                take = pl.ds(part * inner + h * (inner // 2), inner // 2)
+                ga[part, h] = nn(proj_t[take, :], n1[...]).astype(BF).reshape(xs, 2, PIECE, D)
+        for i, by in enumerate(REACH):
+            def sent(i=i, by=by):
+                for hp in range(heads // 2):
+                    home(dkv, hp, by, i).wait_send()
+
+            when(inside(here.me + by, n), sent)
+        dh_out.wait()
+
+    inner_f = heads * 64
+    pl.run_scoped(
+        attention,
+        pltpu.VMEM((window, 128), F32), pltpu.VMEM((window, 128), F32), pltpu.VMEM((span + 128, 128), F32),
+        pltpu.VMEM((inner_f, window), BF), pltpu.VMEM((span + 128, 128), F32), pltpu.VMEM((heads // 2, window, 256), BF),
+        pltpu.VMEM((inner_f, rows), F32), pltpu.VMEM((rows, D), BF), pltpu.VMEM((rows, 3 * inner_f), BF),
+        pltpu.VMEM((3 * inner_f, rows), BF), pltpu.VMEM((rows, D), BF),
+    )
+
+    fold_out = to_partner(ga.at[:, :, :, 1 - c], fold, 2)
+    fold_out.start()
+    def small_to(src, slot, device, i):
+        return pltpu.make_async_remote_copy(
+            src, sland.at[slot], ps.at[i], pr.at[i], device_id=(device,), device_id_type=MESH
+        )
+
+    swap = small_to(small, 0, partner, 0)
+    swap.start()
+    fold_out.wait()
+    for a in range(zs):
+        for b in range(ys):
+            add_into(fold.at[a, b], ga.at[a, b, :, c])
+    fold_in = pltpu.make_async_copy(fold, gr.at[0], osem.at[2])
+    fold_in.start()
+    fold_in.wait()
+    sc.start_load(AT)
+    sc.round(5)
+    swap.wait()
+    small[...] = small[...] + sland[0]
+    swap = small_to(small, 1, here.dev(z, y, 1 - x), 1)
+    swap.start()
+    sc.round(6)
+    swap.wait()
+    small[...] = small[...] + sland[1]
+    swap = small_to(small, 2, here.dev(z, 1 - y, x), 2)
+    swap.start()
+    sc.round(7)
+    swap.wait()
+    small[...] = small[...] + sland[2]
+    swaps = []
+    for far in range(1, zs):
+        swaps.append(small_to(small, 3 + far, here.dev((z + far) % zs, y, x), 2 + far))
+        swaps[-1].start()
+    sc.round(8)
+    for swap in swaps:
+        swap.wait()
+    sland[3] = small[...]
+    ordered = jnp.zeros(small.shape, F32)
+    for plane in range(zs):
+        ordered = ordered + sland[3 + (z - plane + zs) % zs]
+    small[...] = ordered
+    small_out = pltpu.make_async_copy(small, o_small, osem.at[3])
+    small_out.start()
+    for r in range(9, GROUPS + STAGES):
+        sc.round(r)
+    res_out = pltpu.make_async_copy(res, o_res, osem.at[4])
+    res_out.start()
+    res_out.wait()
+    small_out.wait()
+
+
+def backward_call(n, heads, kept, hid, dy, qx, table, rel, na, nf):
+    grads, outp, dn2p, x1, at, q, kv, kx, lse, ga = kept
+    rows, D = hid.shape
+    inner = heads * 64
+    zs, ys, xs = GRIDS[n]
+    window = 5 * rows
+    shape = jax.ShapeDtypeStruct
+    any_, vm = pl.BlockSpec(memory_space=pl.ANY), pl.BlockSpec(memory_space=pltpu.VMEM)
+    sm = pl.BlockSpec(memory_space=pltpu.SMEM)
+    dma = pltpu.SemaphoreType.DMA
+    return pl.pallas_call(
+        functools.partial(backward_kernel, n, heads),
+        out_shape=(
+            shape(grads.shape, BF),
+            shape((rows, D), BF),
+            shape((rows, D), F32),
+            shape((GROUPS, PIECE, D), F32),
+            shape((LINES, 128), F32),
+            shape((rows, D), F32),
+            shape((rows, D), F32),
+        ),
+        in_specs=[any_] * 8 + [vm] + [any_] * 3 + [vm, vm, sm, vm, vm],
+        out_specs=(any_,) * 7,
+        input_output_aliases={0: 0},
+        scratch_shapes=[
+            pltpu.VMEM((WORK, zs, ys, xs, PIECE, D), BF),
+            pltpu.VMEM((SLOTS, zs, PIECE, D), BF),
+            pltpu.VMEM((SLOTS, 5, ys, xs, PIECE, 256), BF),
+            pltpu.VMEM((SLOTS, 5, PIECE, D), BF),
+            pltpu.VMEM((GROUPS, PIECE, D), F32),
+            pltpu.VMEM((rows, D), F32),
+            pltpu.VMEM((window, 2 * inner), BF),
+            pltpu.VMEM((window, 128), BF),
+            pltpu.VMEM((rows, inner), BF),
+            pltpu.VMEM((inner, rows), F32),
+            pltpu.VMEM((zs, ys, xs, 2, PIECE, D), BF),
+            pltpu.VMEM((inner, rows), BF),
+            pltpu.VMEM((rows, inner), BF),
+            pltpu.VMEM((heads // 2, 4, rows, 256), BF),
+            pltpu.VMEM((zs, ys, xs, PIECE, D), BF),
+            pltpu.VMEM((LINES, 128), F32),
+            pltpu.VMEM((3 + zs, LINES, 128), F32),
+            dma((GROUPS, 24)), dma((GROUPS, 24)), dma((GROUPS, 3)),
+            dma((3,)), dma((3,)),
+            dma((heads // 2, 4)), dma((heads // 2, 4)),
+            dma((12,)),
+            dma((3 + zs,)), dma((3 + zs,)),
+            dma((5,)),
+        ],
+        compiler_params=pltpu.CompilerParams(
+            collective_id=2, has_side_effects=True, vmem_limit_bytes=63 * 2**20
+        ),
+        cost_estimate=pl.CostEstimate(flops=12 * 10**9, bytes_accessed=60 * 10**6, transcendentals=10**7),
+        name="backward",
+    )(grads, outp, dn2p, x1, at, q, kv, kx, lse, ga, hid, dy, qx, table, rel, na, nf)
+
+
+def shards(
+    n, hidden, segments, delete_mask, bucket_table, attn_weight, gate_weight, up_weight, down_weight,
+    norm_attn, norm_ffn, rel_bias, out_grad,
+):
+    heads = rel_bias.shape[1]
+    D = hidden.shape[1]
+    slab, kx, qx, table = prepare(
+        hidden, segments, delete_mask, bucket_table, attn_weight, gate_weight, up_weight, down_weight
+    )
+    na, nf = norm_attn[None], norm_ffn[None]
+    kept = forward_call(n, heads, slab, hidden, out_grad, kx, qx, table, rel_bias, na, nf)
+    _, output, d_hidden, res, small, _, _ = backward_call(
+        n, heads, kept, hidden, out_grad, qx, table, rel_bias, na, nf
+    )
+    ffn = res[1:].reshape(GROUPS - 1, 3, 16, D)
+    mats = [ffn[:, i].reshape(-1, D) for i in range(3)]
+    line = lambda first: small[first : first + 12].reshape(-1)[:D]
+    return (
+        output, d_hidden, res[0].T, mats[0].T, mats[1].T, mats[2], line(32), line(44), small[:32, :heads],
+    )
 
 
 def shifted(x, axis, by):
@@ -61,7 +1195,7 @@
     return jnp.where(same_doc, scores, -1e30)
 
 
-def shards(
+def plain_shards(
     hidden,
     segments,
     delete_mask,
@@ -223,33 +1357,18 @@
 
 def solution(mesh):
     placed = (
-        P("seq", None),
-        P("seq"),
-        P("seq"),
-        P(),
-        P(None, "seq"),
-        P(None, "seq"),
-        P(None, "seq"),
-        P("seq", None),
-        P(),
-        P(),
-        P(),
-        P("seq", None),
-    )
+        P("seq", None), P("seq"), P("seq"), P(), P(None, "seq"), P(None, "seq"), P(None, "seq"), P("seq", None),
+        P(), P(), P(), P("seq", None),
+    )
+    n = mesh.shape["seq"]
+    body = functools.partial(shards, n) if n in GRIDS else plain_shards
     return jax.shard_map(
-        shards,
+        body,
         mesh=mesh,
         in_specs=placed,
         out_specs=(
-            P("seq", None),
-            P("seq", None),
-            P(None, "seq"),
-            P(None, "seq"),
-            P(None, "seq"),
-            P("seq", None),
-            P(),
-            P(),
-            P(),
+            P("seq", None), P("seq", None), P(None, "seq"), P(None, "seq"), P(None, "seq"), P("seq", None),
+            P(), P(), P(),
         ),
         check_vma=False,
     )

time: 1440 us -> 525 us (0.36)
  waiting for transfers between devices: 583 us -> 0 us
  Pallas kernels: 0 us -> 499 us
  local copies, waits for them, and re-layouts: 375 us -> 18.6 us
  matrix products: 241 us -> 0 us
  starting transfers between devices: 84.2 us -> 0 us
  other arithmetic: 79.4 us -> 5.75 us
  blocking collectives: 50 us -> 0 us
  between operations: 16.2 us -> 0.75 us
    reduce_scatter x3 -> x0, waiting for transfers between devices: 526 us -> none  [the longest x1 232 us: shards(): lax.psum_scatter(d_w_gate, 'seq', scatter_dimension=1, tiled=True)]
    pallas_call x0 -> x2, Pallas kernels: none -> 499 us  [the longest x1 261 us: forward_call(): pl.pallas_call(functools.partial(forward_kernel, n, heads), out_shape=(sh...]
    dot_general x53 -> x0, matrix products: 241 us -> none  [the longest x17 102 us: matmul_nt(): lax.dot_general(left, right, (((1,), (1,)), ((), ())), preferred_element_...]
    reshape x18 -> x2, local copies, waits for them, and re-layouts: 173 us -> 0.68 us  [the longest x1 0.61 us: shards(): line = lambda first: small[first:first + 12].reshape(-1)[:D]]
    ppermute x24 -> x0, starting transfers between devices: 83.7 us -> none  [shifted(): return lax.ppermute(x, axis, pairs)]
    another operation x13 -> x0, local copies, waits for them, and re-layouts: 73.8 us -> none  [the longest x12 73.6 us: toeplitz(): jnp.tile(line, row_count)[:row_count * (span_len - 1)]]
    pad x12 -> x1, local copies, waits for them, and re-layouts: 58 us -> 0.61 us  [prepare(): table = jnp.pad(table, ((0, 4), (0, 0)), constant_values=-1)]
    psum x1 -> x0, blocking collectives: 50 us -> none  [shards(): s_attn, s_ffn, s_rel = lax.psum((d_norm_attn, d_norm_ffn, d_rel), 'seq')]
  transfers between devices with their start and end apart: 32 -> 0, of which waited for: 7 -> 0; matrix products, arithmetic and copies ran while one was open for 40% -> 0% of each run, Pallas kernels for 0% -> 0%
where the time goes in v1:
time: 525 us; the launch traced here: 524 us
  Pallas kernels  499 us (95%)
  local copies, waits for them, and re-layouts  18.6 us (4%)
  other arithmetic  5.75 us (1%)
    pallas_call x1, Pallas kernels, forward_call(): pl.pallas_call(functools.partial(forward_kernel, n, heads), out_shape=(sh...  261 us
    pallas_call x1, Pallas kernels, backward_call(): pl.pallas_call(functools.partial(backward_kernel, n, heads), out_shape=(s...  239 us
    unnamed x20, local copies, waits for them, and re-layouts  12.4 us

profile of v1, /device:TPU:0, one launch (start us, length us, event | category | flops | bytes accessed | tf_op | source)
XLA Modules:
  0.0 524.3 jit_solution(12927632334070197157)
XLA Ops:
  0.6 0.0 copy-start.4
  0.7 1.3 broadcast_in_dim.91.na
  2.0 1.3 broadcast_in_dim.92.nf
  3.3 0.7 add_select_fusion.3
  4.0 0.8 reverse
  4.8 0.1 slice.48
  4.9 0.1 pad_bitcast_fusion
  4.9 0.6 pad.9.table
  5.6 0.0 copy-start.2
  5.6 1.5 copy.27.rel
  7.0 0.9 select_convert_fusion.qx
  8.0 1.7 select_convert_fusion.1.kx_own
  9.6 1.3 pad_maximum_fusion.1
  10.9 0.0 copy-done.4
  11.0 0.0 copy-start.3
  11.0 1.1 pad_maximum_fusion.slab
  12.1 0.0 copy-done.2
  12.1 1.6 copy.25.hid
  13.7 0.0 copy-done.3
  13.7 1.5 copy.26.dy
  15.2 260.6 %forward.1 = (bf16[8,4,2,2,48,1472]{5,4,3,2,1,0:T(8,128)(2,1)}, f32[1024,1472]{1,0:T(8,128)}, f32[1024,1472]{1,0:T(8,128)}, f32[512,1472]{1,0:T(8,128)}, f32[384...) custom-call(bf16[8,48,1472]{2,1,0:T(8,128)(2,1)} %pad_maximum_fusion, ...), custom_call_target="tpu_custom_call" | custom-call | flops 54999998464 | bytes 80000000 | tf_op jit(solution)/shard_map/forward/pallas_call | solution.py:493
  275.8 238.7 %backward.1 = (bf16[8,4,2,2,48,1472]{5,4,3,2,1,0:T(8,128)(2,1)}, bf16[512,1472]{1,0:T(8,128)(2,1)}, f32[512,1472]{1,0:T(8,128)}, f32[8,48,1472]{2,1,0:T(8,128)},...) custom-call(bf16[8,4,2,2,48,1472]{5,4,3,2,1,0:T(8,128)(2,1)} %get-tuple-eleme, ...), custom_call_target="tpu_custom_call", output_to_operand_aliasing={{0}: (0, {})} | custom-call | flops 12000000000 | bytes 60000000 | tf_op jit(solution)/shard_map/backward/pallas_call | solution.py:1072
  514.5 0.0 copy-start.5
  514.5 0.0 copy-start.1
  514.5 2.7 copy.31
  517.2 0.0 copy-done.5
  517.2 0.7 copy.33
  517.9 0.6 slice_bitcast_fusion.1
  518.5 0.0 copy-done.1
  518.5 0.7 slice_bitcast_fusion
  519.2 0.2 slice.31
  519.4 0.0 copy-start
  519.4 1.4 fusion.3
  520.8 1.3 copy-done
  522.0 2.3 copy.32
  (5 shorter events, 0.0 us)
Async XLA Ops:
  0.6 10.3 %copy-start.4 = (bf16[1472,48]{0,1:T(8,128)(2,1)S(1)}, bf16[1472,48]{0,1:T(8,128)(2,1)}, u32[]{:S(2)}) copy-start(bf16[1472,48]{0,1:T(8,128)(2,1)} %param.16) | copy-start | bytes 423940
  5.6 6.5 %copy-start.2 = (bf16[512,1472]{0,1:T(8,128)(2,1)S(1)}, bf16[512,1472]{0,1:T(8,128)(2,1)}, u32[]{:S(2)}) copy-start(bf16[512,1472]{0,1:T(8,128)(2,1)} %param.12) | copy-start | bytes 4521988
  11.0 2.7 copy-start.3
  514.5 2.7 copy-start.5
  514.5 4.0 copy-start.1
  519.4 2.6 copy-start

commit v2 on v1

--- a/solution.py
+++ b/solution.py
@@ -28,7 +28,7 @@
 
 
 def column_parts(width):
-    return ((0, 256), (256, 640), (896, width - 896))
+    return ((0, 384), (384, 512), (896, width - 896))
 
 
 def when(cond, body):
@@ -133,13 +133,12 @@
     return parts, copy, slot
 
 
-def gather_round(parts, copy, r, ready):
+def gather_visit(parts, copy, v):
     for k in range(STAGES, -1, -1):
-        g = r - k
+        fast = isinstance(v, int) and v == k
+        g = 0 if fast else v - 2 * k
 
         def step(g=g, k=k):
-            if k == 0:
-                ready(g)
             for stages in parts:
                 if k > 0:
                     for move in stages[k - 1]:
@@ -148,11 +147,13 @@
                     for move in stages[k]:
                         when(move[0], lambda move=move: copy(move, g).start())
 
-        if isinstance(r, int):
-            if 0 <= g < GROUPS:
+        if isinstance(v, int):
+            if fast or 0 < g < GROUPS:
                 step()
+            if fast and 0 < v - 2 * k < GROUPS:
+                step(v - 2 * k)
         else:
-            pl.when(inside(g, GROUPS))(step)
+            pl.when((g > 0) & (g < GROUPS))(step)
 
 
 def gather_drain(parts, copy):
@@ -187,7 +188,71 @@
     return lax.rsqrt(jnp.mean(v * v, axis=-1, keepdims=True) + EPS)
 
 
-REACH = (1, -1, 2, -2)
+REACH = (4, -4)
+
+
+class Halo:
+    def __init__(self, here, ref, send, recv):
+        self.here, self.ref, self.send, self.recv = here, ref, send, recv
+        self.rows = ref.shape[-2] // 5
+        even = here.x == 0
+        self.even = even
+        self.partner = here.me + 1 - 2 * here.c
+        self.across = here.me + jnp.where(even, 2, -2)
+        self.near = jnp.where(even, 4, 0)
+        self.far = 4 - self.near
+        step = jnp.where(even, 4, -4)
+        self.to_far = inside(here.me + step, here.n)
+        self.from_far = inside(here.me - step, here.n)
+        self.far_device = jnp.clip(here.me + step, 0, here.n - 1)
+        core0 = here.c == 0
+        self.has_prev, self.has_next = here.me >= 2, here.me < here.n - 2
+        self.over = jnp.where(core0, self.has_next, self.has_prev)
+        self.under = jnp.where(core0, self.has_prev, self.has_next)
+
+    def part(self, slot, piece):
+        at = pl.ds(pl.multiple_of(slot * self.rows, self.rows), self.rows)
+        return self.ref.at[at] if piece is None else self.ref.at[piece, at]
+
+    def move(self, kind, piece):
+        c, j = self.here.c, 0 if piece is None else piece
+        src, dst, device = (
+            (2, self.far, self.across),
+            (self.near, self.far, self.far_device),
+            (2, jnp.where(c == 0, 1, 3), self.partner),
+            (jnp.where(c == 0, 4, 0), jnp.where(c == 0, 3, 1), self.partner),
+        )[kind]
+        return pltpu.make_async_remote_copy(
+            self.part(src, piece), self.part(dst, piece), self.send.at[j, kind], self.recv.at[j, kind],
+            device_id=(device,), device_id_type=MESH,
+        )
+
+    def begin(self, piece=None):
+        self.move(0, piece).start()
+        self.move(2, piece).start()
+
+    def forward(self, piece=None):
+        self.move(0, piece).wait_recv()
+        when(self.to_far, lambda: self.move(1, piece).start())
+
+    def spread(self, piece=None):
+        when(self.from_far, lambda: self.move(1, piece).wait_recv())
+        when(self.over, lambda: self.move(3, piece).start())
+
+    def settle(self, piece=None):
+        self.move(2, piece).wait_recv()
+        when(self.under, lambda: self.move(3, piece).wait_recv())
+
+    def close(self, piece=None):
+        self.move(0, piece).wait_send()
+        self.move(2, piece).wait_send()
+        when(self.to_far, lambda: self.move(1, piece).wait_send())
+        when(self.over, lambda: self.move(3, piece).wait_send())
+
+    def absent(self):
+        core0 = self.here.c == 0
+        no_prev, no_next = jnp.logical_not(self.has_prev), jnp.logical_not(self.has_next)
+        return ((no_prev, 0), (no_next, 4), (no_prev & core0, 1), (no_next & jnp.logical_not(core0), 3))
 
 
 def forward_kernel(
@@ -203,7 +268,7 @@
     inner = qv.shape[1]
     nz = here.grid[0]
     partner = here.me + 1 - 2 * c
-    window = kv.shape[0]
+    window = kx.shape[0]
     tiles = rows // 256
     span = (window - rows) + 256
     mine = pl.ds(pl.multiple_of(c * rows, rows), rows)
@@ -214,25 +279,7 @@
             src, dst, cs.at[i], cr.at[i], device_id=(partner,), device_id_type=MESH
         )
 
-    def halo(ref, by, i, send, recv):
-        return pltpu.make_async_remote_copy(
-            ref.at[centre],
-            ref.at[pl.ds((2 - by) * rows, rows)],
-            send.at[i],
-            recv.at[i],
-            device_id=(jnp.clip(here.me + by, 0, n - 1),),
-            device_id_type=MESH,
-        )
-
-    def halo_each(ref, send, recv, what):
-        for i, by in enumerate(REACH):
-            to, frm = inside(here.me + by, n), inside(here.me - by, n)
-            if what == "start":
-                when(to, lambda i=i, by=by: halo(ref, by, i, send, recv).start())
-            elif what == "recv":
-                when(frm, lambda i=i, by=by: halo(ref, by, i, send, recv).wait_recv())
-            else:
-                when(to, lambda i=i, by=by: halo(ref, by, i, send, recv).wait_send())
+    kv_halo, kx_halo = Halo(here, kv, hs, hr), Halo(here, kx, ks, kr)
 
     own = [
         pltpu.make_async_copy(slab.at[g], G.at[g, here.z, here.y, here.x], lsem.at[g])
@@ -248,20 +295,22 @@
     for copy in own:
         copy.wait()
     parts, copy, _ = gather_stages(here, G, gs, gr, D)
-    ag = lambda r: gather_round(parts, copy, r, lambda g: None)
+    ag = lambda v: gather_visit(parts, copy, v)
     ag(0)
     kx_in.wait()
-    halo_each(kx, ks, kr, "start")
+    kx_halo.begin()
     dy_in.wait()
     dy_out = to_partner(dyf.at[mine], dyf.at[mine], 0)
     dy_out.start()
     edge = jnp.where(lax.broadcasted_iota(jnp.int32, (rows, 128), 1) == 25, -BIG, 0.0).astype(BF)
-    for by in REACH:
-        def absent(by=by):
-            at_rows = pl.ds((2 - by) * rows, rows)
-            kv[at_rows, :] = jnp.zeros((rows, kv.shape[1]), BF)
+    for cond, slot in kv_halo.absent():
+        def absent(slot=slot):
+            at_rows = pl.ds(slot * rows, rows)
             kx[at_rows, :] = edge
-        pl.when(jnp.logical_not(inside(here.me - by, n)))(absent)
+            for hp in range(heads // 2):
+                kv[hp, at_rows, :] = jnp.zeros((rows, 256), BF)
+
+        pl.when(cond)(absent)
 
     def attention(n1, bias, vt, S, Pm):
         ag(1)
@@ -274,7 +323,7 @@
 
         lax.fori_loop(0, rows // 64, norm_rows, 0)
         ag(2)
-        lines = table.shape[0]
+        kx_halo.forward()
         for head in range(heads):
             line = shift_line(table[...], rel, head)
             for b in range(bias.shape[1] // 128):
@@ -284,8 +333,10 @@
                 bias[head, 128 * b : 128 * b + 128, :] = pltpu.roll(both, 0, 1, stride=1, stride_axis=0)[:, :128]
             if head == 1:
                 ag(3)
+                kx_halo.spread()
             if head == 3:
                 ag(4)
+                kx_halo.settle()
         ag(5)
         keep = pltpu.make_async_copy(G.at[0], ga.at[:, :, :, c], lsem.at[GROUPS + 2])
         keep.start()
@@ -303,35 +354,46 @@
                 got = nt(n1[at_rows, :], weight).astype(BF)
                 if part == 0:
                     qv[at_rows, :] = got
-                else:
-                    kv[pl.ds(2 * rows + 256 * half, 256), (part - 1) * inner : part * inner] = got
-        halo_each(kv, hs, hr, "start")
-        ag(6)
-        halo_each(kx, ks, kr, "recv")
-        halo_each(kv, hs, hr, "recv")
-        kv_out = pltpu.make_async_copy(kv, o_kv, osem.at[2])
-        kv_out.start()
+                    continue
+                for hp in range(heads // 2):
+                    kv[hp, pl.ds(2 * rows + 256 * half, 256), 128 * (part - 1) : 128 * part] = got[
+                        :, 128 * hp : 128 * hp + 128
+                    ]
+            if part == 2:
+                for hp in range(heads // 2):
+                    kv_halo.begin(hp)
         kx_out = pltpu.make_async_copy(kx, o_kx, osem.at[3])
         kx_out.start()
         q_out = pltpu.make_async_copy(qv, o_q, osem.at[4])
         q_out.start()
-
-        def turn(i, _):
-            at_rows = pl.ds(pl.multiple_of(i * 256, 256), 256)
-            vt[:, at_rows] = kv[at_rows, inner:].T
-            return 0
-
-        lax.fori_loop(0, window // 256, turn, 0)
+        ag(6)
+        kv_halo.forward(0)
+        ag(7)
+        kv_halo.forward(1)
+        kv_halo.spread(0)
+        kv_halo.forward(2)
+        kv_halo.settle(0)
         lane = lax.broadcasted_iota(jnp.int32, (256, 128), 1) // 64
 
         def pair(hp, _):
             @pl.when(hp > 0)
             def _():
-                ag(hp + 6)
+                kv_halo.settle(hp)
 
             cols = pl.ds(pl.multiple_of(hp * 128, 128), 128)
 
+            def turn(i, _):
+                at_rows = pl.ds(pl.multiple_of(i * 256, 256), 256)
+                vt[:, at_rows] = kv[hp, at_rows, 128:256].T
+                return 0
+
+            lax.fori_loop(0, window // 256, turn, 0)
+
             def one(k, _):
+                @pl.when(k == 1)
+                def _():
+                    ag(8 + hp)
+
                 t, e = k // 2, k % 2
                 base = pl.multiple_of(t * 256, 256)
                 head = hp * 2 + e
@@ -341,7 +403,7 @@
 
                 def score(b, m):
                     at_rows = pl.ds(pl.multiple_of(base + b * 256, 256), 256)
-                    ka = jnp.concatenate([kv[at_rows, cols], kx[at_rows, :]], 1)
+                    ka = jnp.concatenate([kv[hp, at_rows, 0:128], kx[at_rows, :]], 1)
                     s = nt(ka, qa)
                     low = pl.multiple_of(b * 256, 256)
                     plane = jnp.concatenate(
@@ -351,7 +413,7 @@
                     S[pl.ds(low, 256), :] = s
                     return jnp.maximum(m, jnp.max(s.reshape(32, 8, 256), axis=0))
 
-                m = lax.fori_loop(0, span // 256, score, jnp.full((8, 256), -3e38, F32))
+                m = lax.fori_loop(0, span // 256, score, jnp.full((8, 256), -3e38, F32), unroll=True)
                 m = jnp.max(m, axis=0, keepdims=True)
 
                 def weigh(b, total):
@@ -360,18 +422,25 @@
                     Pm[at_rows, :] = p.astype(BF)
                     return total + jnp.sum(p.reshape(32, 8, 256), axis=0)
 
-                total = lax.fori_loop(0, span // 256, weigh, jnp.zeros((8, 256), F32))
+                total = lax.fori_loop(0, span // 256, weigh, jnp.zeros((8, 256), F32), unroll=True)
                 total = jnp.sum(total, axis=0, keepdims=True)
                 out_rows = pl.ds(pl.multiple_of(head * 64, 64), 64)
-                mixed = nn(vt[out_rows, pl.ds(base, span)], Pm[...])
+                mixed = nn(vt[pl.ds(pl.multiple_of(e * 64, 64), 64), pl.ds(base, span)], Pm[...])
                 at[out_rows, pl.ds(base, 256)] = mixed / total
                 lse[pl.ds(head, 1), pl.ds(base, 256)] = m + jnp.log(total)
                 return 0
 
             lax.fori_loop(0, 2 * tiles, one, 0)
+
+            @pl.when(hp < heads // 2 - 1)
+            def _():
+                kv_halo.spread(hp + 1)
+
             return 0
 
         lax.fori_loop(0, heads // 2, pair, 0)
+        kv_out = pltpu.make_async_copy(kv, o_kv, osem.at[2])
+        kv_out.start()
         outs = [
             pltpu.make_async_copy(at, o_at, osem.at[5]),
             pltpu.make_async_copy(lse, o_lse, osem.at[6]),
@@ -396,8 +465,9 @@
         give.wait_send()
         n2_out.wait()
         dy_out.wait()
-        halo_each(kx, ks, kr, "send")
-        halo_each(kv, hs, hr, "send")
+        kx_halo.close()
+        for hp in range(heads // 2):
+            kv_halo.close(hp)
         for o in outs + [ga_out, kv_out, kx_out, q_out, x1_out]:
             o.wait()
 
@@ -405,7 +475,7 @@
         attention,
         pltpu.VMEM((rows, D), BF),
         pltpu.VMEM((heads, span + 128, 128), F32),
-        pltpu.VMEM((inner, window), BF),
+        pltpu.VMEM((128, window), BF),
         pltpu.VMEM((span, 256), F32),
         pltpu.VMEM((span, 256), BF),
     )
@@ -418,7 +488,7 @@
             return pltpu.make_async_copy(stage.at[j % 2], o_grads.at[j + 1], stsem.at[j % 2])
 
         def chunk(j, _):
-            ag(j + 9)
+            ag(j + 11)
             g = j + 1
             wg = G.at[g, :, :, :, pl.ds(0, 16), :]
             wu = G.at[g, :, :, :, pl.ds(16, 16), :]
@@ -442,7 +512,7 @@
                 acc_n[at_rows, :] += nn(dg.T, whole(wg)) + nn(du.T, whole(wu))
                 return 0
 
-            lax.fori_loop(0, 2 * rows // 256, tokens, 0)
+            lax.fori_loop(0, 2 * rows // 256, tokens, 0, unroll=2)
 
             @pl.when(j >= 2)
             def _():
@@ -499,7 +569,7 @@
             shape((rows, D), F32),
             shape((inner, rows), F32),
             shape((rows, inner), BF),
-            shape((window, 2 * inner), BF),
+            shape((heads // 2, window, 256), BF),
             shape((window, 128), BF),
             shape((8, rows), F32),
             shape((zs, ys, xs, 2, PIECE, D), BF),
@@ -511,7 +581,7 @@
             pltpu.VMEM((zs, ys, xs, 2, PIECE, D), BF),
             pltpu.VMEM((2 * rows, D), BF),
             pltpu.VMEM((2 * rows, D), BF),
-            pltpu.VMEM((window, 2 * inner), BF),
+            pltpu.VMEM((heads // 2, window, 256), BF),
             pltpu.VMEM((window, 128), BF),
             pltpu.VMEM((rows, inner), BF),
             pltpu.VMEM((rows, D), F32),
@@ -519,7 +589,7 @@
             pltpu.VMEM((8, rows), F32),
             dma((GROUPS, slots)), dma((GROUPS, slots)),
             dma((GROUPS + 3,)),
-            dma((4,)), dma((4,)), dma((4,)), dma((4,)),
+            dma((heads // 2, 4)), dma((heads // 2, 4)), dma((1, 4)), dma((1, 4)),
             dma((3,)), dma((3,)),
             dma((8,)), dma((2,)),
         ],
@@ -551,17 +621,19 @@
     return slab, kx, qx, table
 
 
-FIRST = (1, 2, 3, 4, 5, 0, 6, 7)
-AT = 5
-SLOTS = 3
-WORK = 6
+FIRST = (1, 2, 3, 4, 5, 6, 7, 0)
+AT = 7
+AFTER = 11
+SLOTS = 4
+ZSLOTS = 6
+WORK = 8
 LINES = 56
 
 
 def group_of(pos):
     if isinstance(pos, int):
         return FIRST[pos]
-    return jnp.where(pos < AT, pos + 1, jnp.where(pos == AT, 0, pos))
+    return (pos + 1) % GROUPS
 
 
 def add_into(dst, src):
@@ -598,7 +670,7 @@
         cols = pl.ds(*self.parts[part])
         dim = (("z0", "z1", "z2", "y", "x"), ("y", "x", "z0", "z1", "z2"), ("x", "y", "z0", "z1", "z2"))[part][k]
         work, source, g = self.work, self.source, group_of(pos)
-        w, slot = pos % WORK, pos % SLOTS
+        w, slot, zslot = pos % WORK, pos % SLOTS, pos % ZSLOTS
         base = 8 * part
 
         def remote(src, dst, at, device):
@@ -618,9 +690,9 @@
                 device = here.dev(jnp.clip(z + way, 0, zs - 1), y, x)
                 block, mine = jnp.clip(target, 0, zs - 1), jnp.clip(got, 0, zs - 1)
                 if part == 0:
-                    src, dst = work.at[w, block, :, :, :, cols], self.landa.at[slot, spot]
+                    src, dst = work.at[w, block, :, :, :, cols], self.landa.at[zslot, spot]
                 else:
-                    src, dst = work.at[w, block, y, x, :, cols], self.landz.at[slot, spot, :, cols]
+                    src, dst = work.at[w, block, y, x, :, cols], self.landz.at[zslot, spot, :, cols]
 
                 def consume(mine=mine, dst=dst):
                     if part == 0:
@@ -671,13 +743,13 @@
         if part == 0:
             self.result[g, :, cols] = own + self.land[slot, xs, :, cols].astype(F32)
             return
-        up = self.landz[slot, zs - 2, :, cols].astype(F32)
-        down = self.landz[slot, zs, :, cols].astype(F32)
+        up = self.landz[pos % ZSLOTS, zs - 2, :, cols].astype(F32)
+        down = self.landz[pos % ZSLOTS, zs, :, cols].astype(F32)
         self.result[g, :, cols] = own + jnp.where(z > 0, up, 0.0) + jnp.where(z < zs - 1, down, 0.0)
 
     def round(self, r):
         for k in range(STAGES, -1, -1):
-            pos = r - k
+            pos = r - 2 * k
 
             def step(pos=pos, k=k):
                 for part in range(3):
@@ -698,14 +770,14 @@
                     for stage in range(STAGES):
                         for sends, _, copy, _ in self.moves(part, stage, pos):
                             when(sends, lambda copy=copy: copy.wait_send())
-                if k == STAGES:
-                    when(pos + WORK < GROUPS, lambda: self.start_load(pos + WORK))
 
             if isinstance(pos, int):
-                if 0 <= pos < GROUPS:
+                if 0 <= pos < GROUPS - 1:
                     step()
             else:
-                pl.when(inside(pos, GROUPS))(step)
+                pl.when(inside(pos, GROUPS - 1))(step)
+            if isinstance(r, int) and r - AFTER == k:
+                step(AT, k)
 
 
 def norm_back(v, gain, d):
@@ -734,7 +806,7 @@
     c = here.c
     rows, D = dx1.shape
     inner = qv.shape[1]
-    window = kv.shape[0]
+    window = kx.shape[0]
     zs, ys, xs = here.grid
     z, y, x = here.z, here.y, here.x
     span = window - rows + 256
@@ -775,6 +847,7 @@
         dn_out.wait_recv()
         second = local(dn_land, other, 8)
         second.start()
+        sc.round(1)
         for load in loads + first + [second]:
             load.wait()
         w_out = ga[zs - 1].reshape(inner, D)
@@ -796,7 +869,7 @@
         put_line(small, 44, jnp.sum(total, axis=0, keepdims=True))
         third = local(outp.at[mine], other, 9)
         third.start()
-        sc.round(1)
+        sc.round(2)
         for h in range(2):
             part = nn(at[pl.ds(h * (inner // 2), inner // 2), :].astype(BF), low[...])
             ga[zs - 1, h] = part.astype(BF).reshape(xs, 2, PIECE, D)
@@ -830,26 +903,55 @@
         pltpu.VMEM((rows, D), BF),
     )
 
-    def home(dkv, hp, by, i):
+    way = Halo(here, kx, hs, hr)
+
+    def home(dkv, hp, kind):
+        src, device = (
+            (jnp.where(c == 0, 1, 3), partner),
+            (jnp.where(c == 0, 3, 1), partner),
+            (way.far, jnp.clip(here.me - jnp.where(way.even, 4, -4), 0, n - 1)),
+            (way.near, way.across),
+        )[kind]
         return pltpu.make_async_remote_copy(
-            dkv.at[hp, pl.ds((2 + by) * rows, rows)],
-            back.at[hp, i],
-            hs.at[hp, i],
-            hr.at[hp, i],
-            device_id=(jnp.clip(here.me + by, 0, n - 1),),
+            dkv.at[hp, pl.ds(pl.multiple_of(src * rows, rows), rows)],
+            back.at[hp, kind],
+            hs.at[hp, kind],
+            hr.at[hp, kind],
+            device_id=(device,),
             device_id_type=MESH,
         )
 
-    def attention(acc_k, acc_v, skew, kt, bias, dkv, dqt, n1, proj, proj_t, hid_v):
-        hid_in = local(hid, hid_v, 11)
-        hid_in.start()
-
-        def turn(i, _):
-            at_rows = pl.ds(pl.multiple_of(i * 256, 256), 256)
-            kt[:, at_rows] = kv[at_rows, 0:inner].T
-            return 0
-
-        lax.fori_loop(0, window // 256, turn, 0)
+    def add_back(dkv, hp, kind, slot):
+        at_rows = pl.ds(pl.multiple_of(slot * rows, rows), rows)
+        add_into(dkv.at[hp, at_rows], back.at[hp, kind])
+
+    def home_begin(dkv, hp):
+        when(way.under, lambda: home(dkv, hp, 0).start())
+        home(dkv, hp, 1).start()
+
+    def home_merge(dkv, hp):
+        def merge():
+            home(dkv, hp, 0).wait_recv()
+            add_back(dkv, hp, 0, jnp.where(c == 0, 4, 0))
+
+        when(way.over, merge)
+        when(way.from_far, lambda: home(dkv, hp, 2).start())
+
+    def home_cross(dkv, hp):
+        def merge():
+            home(dkv, hp, 2).wait_recv()
+            add_back(dkv, hp, 2, way.near)
+
+        when(way.to_far, merge)
+        home(dkv, hp, 3).start()
+
+    def home_close(dkv, hp):
+        when(way.under, lambda: home(dkv, hp, 0).wait_send())
+        home(dkv, hp, 1).wait_send()
+        when(way.from_far, lambda: home(dkv, hp, 2).wait_send())
+        home(dkv, hp, 3).wait_send()
+
+    def pairs(dkv, dqt, acc_k, acc_v, skew, kt, bias):
         dqt[...] = jnp.zeros_like(dqt)
         lane = lax.broadcasted_iota(jnp.int32, (256, 128), 1) // 64
         lane_of = lax.broadcasted_iota(jnp.int32, (32, 128), 1)
@@ -857,8 +959,8 @@
 
         def one_head(hp, e):
             head = hp * 2 + e
+            pl.when(e == 0)(lambda: sc.round(3 + hp))
             cols = pl.ds(pl.multiple_of(hp * 128, 128), 128)
-            vcols = pl.ds(pl.multiple_of(inner + hp * 128, 128), 128)
             out_rows = pl.ds(pl.multiple_of(head * 64, 64), 64)
             line = shift_line(table[...], rel, head)
             for b in range(blocks):
@@ -881,18 +983,18 @@
                 def block(b, dq):
                     low = pl.multiple_of(b * 256, 256)
                     at_rows = pl.ds(pl.multiple_of(base + b * 256, 256), 256)
-                    ka = jnp.concatenate([kv[at_rows, cols], kx[at_rows, :]], 1)
+                    ka = jnp.concatenate([kv[hp, at_rows, 0:128], kx[at_rows, :]], 1)
                     plane = jnp.concatenate([bias[pl.ds(low + 128, 256), :], bias[pl.ds(low, 256), :]], 1)
                     p = jnp.exp(nt(ka, qa) + plane - logs)
-                    ds = p * (nt(kv[at_rows, vcols], da) - delta)
+                    ds = p * (nt(kv[hp, at_rows, 128:256], da) - delta)
                     skew[pl.ds(low + 128, 256), :] += ds[:, 0:128]
                     skew[pl.ds(low, 256), :] += ds[:, 128:256]
                     dsr = ds.astype(BF)
                     acc_v[at_rows, :] += nn(p.astype(BF), da)
                     acc_k[at_rows, :] += nn(dsr, q)
-                    return dq + nn(kt[out_rows, at_rows], dsr)
-
-                dqt[out_rows, here_q] = lax.fori_loop(0, span // 256, block, jnp.zeros((64, 256), F32))
+                    return dq + nn(kt[pl.ds(pl.multiple_of(e * 64, 64), 64), at_rows], dsr)
+
+                dqt[out_rows, here_q] = lax.fori_loop(0, span // 256, block, jnp.zeros((64, 256), F32), unroll=True)
                 return 0
 
             lax.fori_loop(0, rows // 256, tile, 0)
@@ -913,9 +1015,15 @@
             small[0:32, :] = jnp.where(lane_of == head, sums, small[0:32, :])
 
         def pair(hp, _):
-            sc.round(hp + 2)
             acc_k[...] = jnp.zeros_like(acc_k)
             acc_v[...] = jnp.zeros_like(acc_v)
+
+            def turn(i, _):
+                at_rows = pl.ds(pl.multiple_of(i * 256, 256), 256)
+                kt[:, at_rows] = kv[hp, at_rows, 0:128].T
+                return 0
+
+            lax.fori_loop(0, window // 256, turn, 0)
             lax.fori_loop(0, 2, lambda e, _: (one_head(hp, e), 0)[1], 0)
 
             def pack(i, _):
@@ -925,11 +1033,20 @@
                 return 0
 
             lax.fori_loop(0, window // 128, pack, 0)
-            for i, by in enumerate(REACH):
-                when(inside(here.me + by, n), lambda i=i, by=by: home(dkv, hp, by, i).start())
+            home_begin(dkv, hp)
+            pl.when(hp >= 1)(lambda: home_merge(dkv, hp - 1))
+            pl.when(hp >= 2)(lambda: home_cross(dkv, hp - 2))
             return 0
 
         lax.fori_loop(0, heads // 2, pair, 0)
+        last = heads // 2 - 1
+        home_cross(dkv, last - 1)
+        home_merge(dkv, last)
+        sc.round(6)
+
+    def to_weights(dkv, dqt, n1, proj, proj_t, hid_v):
+        hid_in = local(hid, hid_v, 11)
+        hid_in.start()
         hid_in.wait()
 
         def norm_rows(i, _):
@@ -941,19 +1058,13 @@
         lax.fori_loop(0, rows // 64, norm_rows, 0)
 
         def gather_pair(hp, _):
-            for i, by in enumerate(REACH):
-                frm = inside(here.me - by, n)
-                when(frm, lambda i=i, by=by: home(dkv, hp, by, i).wait_recv())
-
-                def absent(i=i):
-                    back[hp, i] = jnp.zeros((rows, 256), BF)
-
-                when(jnp.logical_not(frm), absent)
+            home(dkv, hp, 1).wait_recv()
+            home(dkv, hp, 3).wait_recv()
 
             def sum_rows(j, _):
                 at_rows = pl.ds(pl.multiple_of(j * 128, 128), 128)
                 total = dkv[hp, pl.ds(pl.multiple_of(2 * rows + j * 128, 128), 128), :].astype(F32)
-                for i in range(4):
+                for i in (1, 3):
                     total = total + back[hp, i, at_rows, :].astype(F32)
                 total = total.astype(BF)
                 for part in range(2):
@@ -970,7 +1081,12 @@
             lax.fori_loop(0, rows // 128, sum_rows, 0)
             return 0
 
-        lax.fori_loop(0, heads // 2, gather_pair, 0)
+        last = heads // 2 - 1
+        sc.round(7)
+        lax.fori_loop(0, last, gather_pair, 0)
+        home_cross(dkv, last)
+        sc.round(8)
+        gather_pair(last, 0)
 
         def to_hidden(i, total):
             at_rows = pl.ds(pl.multiple_of(i * 128, 128), 128)
@@ -985,27 +1101,29 @@
         put_line(small, 32, jnp.sum(total, axis=0, keepdims=True))
         dh_out = pltpu.make_async_copy(dx1, o_dh, osem.at[1])
         dh_out.start()
+        sc.round(9)
 
         for part in range(3):
             for h in range(2):
                 take = pl.ds(part * inner + h * (inner // 2), inner // 2)
                 ga[part, h] = nn(proj_t[take, :], n1[...]).astype(BF).reshape(xs, 2, PIECE, D)
-        for i, by in enumerate(REACH):
-            def sent(i=i, by=by):
-                for hp in range(heads // 2):
-                    home(dkv, hp, by, i).wait_send()
-
-            when(inside(here.me + by, n), sent)
+        for hp in range(heads // 2):
+            home_close(dkv, hp)
         dh_out.wait()
 
-    inner_f = heads * 64
-    pl.run_scoped(
-        attention,
-        pltpu.VMEM((window, 128), F32), pltpu.VMEM((window, 128), F32), pltpu.VMEM((span + 128, 128), F32),
-        pltpu.VMEM((inner_f, window), BF), pltpu.VMEM((span + 128, 128), F32), pltpu.VMEM((heads // 2, window, 256), BF),
-        pltpu.VMEM((inner_f, rows), F32), pltpu.VMEM((rows, D), BF), pltpu.VMEM((rows, 3 * inner_f), BF),
-        pltpu.VMEM((3 * inner_f, rows), BF), pltpu.VMEM((rows, D), BF),
-    )
+    def attention(dkv, dqt):
+        pl.run_scoped(
+            functools.partial(pairs, dkv, dqt),
+            pltpu.VMEM((window, 128), F32), pltpu.VMEM((window, 128), F32), pltpu.VMEM((span + 128, 128), F32),
+            pltpu.VMEM((128, window), BF), pltpu.VMEM((span + 128, 128), F32),
+        )
+        pl.run_scoped(
+            functools.partial(to_weights, dkv, dqt),
+            pltpu.VMEM((rows, D), BF), pltpu.VMEM((rows, 3 * inner), BF), pltpu.VMEM((3 * inner, rows), BF),
+            pltpu.VMEM((rows, D), BF),
+        )
+
+    pl.run_scoped(attention, pltpu.VMEM((heads // 2, window, 256), BF), pltpu.VMEM((inner, rows), F32))
 
     fold_out = to_partner(ga.at[:, :, :, 1 - c], fold, 2)
     fold_out.start()
@@ -1016,6 +1134,7 @@
 
     swap = small_to(small, 0, partner, 0)
     swap.start()
+    sc.round(10)
     fold_out.wait()
     for a in range(zs):
         for b in range(ys):
@@ -1024,24 +1143,24 @@
     fold_in.start()
     fold_in.wait()
     sc.start_load(AT)
-    sc.round(5)
+    sc.round(11)
     swap.wait()
     small[...] = small[...] + sland[0]
     swap = small_to(small, 1, here.dev(z, y, 1 - x), 1)
     swap.start()
-    sc.round(6)
+    sc.round(12)
     swap.wait()
     small[...] = small[...] + sland[1]
     swap = small_to(small, 2, here.dev(z, 1 - y, x), 2)
     swap.start()
-    sc.round(7)
+    sc.round(13)
     swap.wait()
     small[...] = small[...] + sland[2]
     swaps = []
     for far in range(1, zs):
         swaps.append(small_to(small, 3 + far, here.dev((z + far) % zs, y, x), 2 + far))
         swaps[-1].start()
-    sc.round(8)
+    sc.round(14)
     for swap in swaps:
         swap.wait()
     sland[3] = small[...]
@@ -1051,7 +1170,7 @@
     small[...] = ordered
     small_out = pltpu.make_async_copy(small, o_small, osem.at[3])
     small_out.start()
-    for r in range(9, GROUPS + STAGES):
+    for r in range(15, GROUPS - 1 + 2 * STAGES):
         sc.round(r)
     res_out = pltpu.make_async_copy(res, o_res, osem.at[4])
     res_out.start()
@@ -1086,11 +1205,11 @@
         scratch_shapes=[
             pltpu.VMEM((WORK, zs, ys, xs, PIECE, D), BF),
             pltpu.VMEM((SLOTS, zs, PIECE, D), BF),
-            pltpu.VMEM((SLOTS, 5, ys, xs, PIECE, 256), BF),
-            pltpu.VMEM((SLOTS, 5, PIECE, D), BF),
+            pltpu.VMEM((ZSLOTS, 5, ys, xs, PIECE, 384), BF),
+            pltpu.VMEM((ZSLOTS, 5, PIECE, D), BF),
             pltpu.VMEM((GROUPS, PIECE, D), F32),
             pltpu.VMEM((rows, D), F32),
-            pltpu.VMEM((window, 2 * inner), BF),
+            pltpu.VMEM((heads // 2, window, 256), BF),
             pltpu.VMEM((window, 128), BF),
             pltpu.VMEM((rows, inner), BF),
             pltpu.VMEM((inner, rows), F32),

time: 525 us -> 425 us (0.81)
  Pallas kernels: 499 us -> 398 us
    pallas_call x1, Pallas kernels: 261 us -> 202 us  [forward_call(): pl.pallas_call(functools.partial(forward_kernel, n, heads), out_shape=(sh...]
    pallas_call x1, Pallas kernels: 239 us -> 197 us  [backward_call(): pl.pallas_call(functools.partial(backward_kernel, n, heads), out_shape=(s...]
where the time goes in v2:
time: 425 us; the launch traced here: 423 us
  Pallas kernels  398 us (94%)
  local copies, waits for them, and re-layouts  18.6 us (4%)
  other arithmetic  5.75 us (1%)
    pallas_call x1, Pallas kernels, forward_call(): pl.pallas_call(functools.partial(forward_kernel, n, heads), out_shape=(sh...  202 us
    pallas_call x1, Pallas kernels, backward_call(): pl.pallas_call(functools.partial(backward_kernel, n, heads), out_shape=(s...  197 us
    unnamed x20, local copies, waits for them, and re-layouts  12.4 us

profile of v2, /device:TPU:0, one launch (start us, length us, event | category | flops | bytes accessed | tf_op | source)
XLA Modules:
  0.0 423.2 jit_solution(11284506488999557219)
XLA Ops:
  0.6 0.0 copy-start.4
  0.7 1.3 broadcast_in_dim.91.na
  2.0 1.3 broadcast_in_dim.92.nf
  3.3 0.7 add_select_fusion.3
  4.0 0.8 reverse
  4.8 0.1 slice.48
  4.9 0.1 pad_bitcast_fusion
  4.9 0.6 pad.9.table
  5.6 0.0 copy-start.2
  5.6 1.5 copy.27.rel
  7.0 0.9 select_convert_fusion.qx
  8.0 1.7 select_convert_fusion.1.kx_own
  9.6 1.3 pad_maximum_fusion.1
  10.9 0.0 copy-done.4
  11.0 0.0 copy-start.3
  11.0 1.1 pad_maximum_fusion.slab
  12.1 0.0 copy-done.2
  12.1 1.6 copy.25.hid
  13.7 0.0 copy-done.3
  13.7 1.5 copy.26.dy
  15.2 201.5 %forward.1 = (bf16[8,4,2,2,48,1472]{5,4,3,2,1,0:T(8,128)(2,1)}, f32[1024,1472]{1,0:T(8,128)}, f32[1024,1472]{1,0:T(8,128)}, f32[512,1472]{1,0:T(8,128)}, f32[384...) custom-call(bf16[8,48,1472]{2,1,0:T(8,128)(2,1)} %pad_maximum_fusion, ...), custom_call_target="tpu_custom_call" | custom-call | flops 54999998464 | bytes 80000000 | tf_op jit(solution)/shard_map/forward/pallas_call | solution.py:563
  216.7 196.6 %backward.1 = (bf16[8,4,2,2,48,1472]{5,4,3,2,1,0:T(8,128)(2,1)}, bf16[512,1472]{1,0:T(8,128)(2,1)}, f32[512,1472]{1,0:T(8,128)}, f32[8,48,1472]{2,1,0:T(8,128)},...) custom-call(bf16[8,4,2,2,48,1472]{5,4,3,2,1,0:T(8,128)(2,1)} %get-tuple-eleme, ...), custom_call_target="tpu_custom_call", output_to_operand_aliasing={{0}: (0, {})} | custom-call | flops 12000000000 | bytes 60000000 | tf_op jit(solution)/shard_map/backward/pallas_call | solution.py:1191
  413.3 0.0 copy-start.5
  413.3 0.0 copy-start.1
  413.3 2.7 copy.31
  416.0 0.0 copy-done.5
  416.0 0.7 copy.33
  416.7 0.6 slice_bitcast_fusion.1
  417.3 0.0 copy-done.1
  417.3 0.7 slice_bitcast_fusion
  418.1 0.2 slice.31
  418.2 0.0 copy-start
  418.2 1.4 fusion.3
  419.6 1.3 copy-done
  420.9 2.3 copy.32
  (5 shorter events, 0.0 us)
Async XLA Ops:
  0.6 10.3 %copy-start.4 = (bf16[1472,48]{0,1:T(8,128)(2,1)S(1)}, bf16[1472,48]{0,1:T(8,128)(2,1)}, u32[]{:S(2)}) copy-start(bf16[1472,48]{0,1:T(8,128)(2,1)} %param.16) | copy-start | bytes 423940
  5.6 6.5 %copy-start.2 = (bf16[512,1472]{0,1:T(8,128)(2,1)S(1)}, bf16[512,1472]{0,1:T(8,128)(2,1)}, u32[]{:S(2)}) copy-start(bf16[512,1472]{0,1:T(8,128)(2,1)} %param.12) | copy-start | bytes 4521988
  11.0 2.7 copy-start.3
  413.3 2.7 copy-start.5
  413.3 4.0 copy-start.1
  418.2 2.6 copy-start

commit v3 on v2

--- a/solution.py
+++ b/solution.py
@@ -15,6 +15,8 @@
 ORDERS = ("xyz", "zxy", "zyx")
 GROUPS = 8
 STAGES = 5
+GATHER_DELAY = ((0, 2, 4, 5, 6, 7), (0, 1, 2, 3, 5, 7), (0, 1, 2, 3, 5, 7))
+SCATTER_DELAY = ((0, 1, 2, 3, 5, 7), (0, 2, 4, 5, 6, 7), (0, 2, 4, 5, 6, 7))
 PIECE = 48
 EPS = 1e-06
 
@@ -135,11 +137,9 @@
 
 def gather_visit(parts, copy, v):
     for k in range(STAGES, -1, -1):
-        fast = isinstance(v, int) and v == k
-        g = 0 if fast else v - 2 * k
-
-        def step(g=g, k=k):
-            for stages in parts:
+        for part, stages in enumerate(parts):
+
+            def step(g, k=k, stages=stages):
                 if k > 0:
                     for move in stages[k - 1]:
                         when(move[1], lambda move=move: copy(move, g).wait_recv())
@@ -147,13 +147,14 @@
                     for move in stages[k]:
                         when(move[0], lambda move=move: copy(move, g).start())
 
-        if isinstance(v, int):
-            if fast or 0 < g < GROUPS:
-                step()
-            if fast and 0 < v - 2 * k < GROUPS:
-                step(v - 2 * k)
-        else:
-            pl.when((g > 0) & (g < GROUPS))(step)
+            g = v - GATHER_DELAY[part][k]
+            if not isinstance(v, int):
+                pl.when((g > 0) & (g < GROUPS))(functools.partial(step, g))
+                continue
+            if v == k:
+                step(0)
+            if 0 < g < GROUPS:
+                step(g)
 
 
 def gather_drain(parts, copy):
@@ -368,7 +369,6 @@
         q_out.start()
         ag(6)
         kv_halo.forward(0)
-        ag(7)
         kv_halo.forward(1)
         kv_halo.spread(0)
         kv_halo.forward(2)
@@ -390,9 +390,9 @@
             lax.fori_loop(0, window // 256, turn, 0)
 
             def one(k, _):
-                @pl.when(k == 1)
+                @pl.when((k == 1) & (hp == 1))
                 def _():
-                    ag(8 + hp)
+                    ag(7)
 
                 t, e = k // 2, k % 2
                 base = pl.multiple_of(t * 256, 256)
@@ -488,7 +488,7 @@
             return pltpu.make_async_copy(stage.at[j % 2], o_grads.at[j + 1], stsem.at[j % 2])
 
         def chunk(j, _):
-            ag(j + 11)
+            ag(j + 8)
             g = j + 1
             wg = G.at[g, :, :, :, pl.ds(0, 16), :]
             wu = G.at[g, :, :, :, pl.ds(16, 16), :]
@@ -623,9 +623,9 @@
 
 FIRST = (1, 2, 3, 4, 5, 6, 7, 0)
 AT = 7
-AFTER = 11
+AFTER = 10
 SLOTS = 4
-ZSLOTS = 6
+ZSLOTS = 4
 WORK = 8
 LINES = 56
 
@@ -749,10 +749,9 @@
 
     def round(self, r):
         for k in range(STAGES, -1, -1):
-            pos = r - 2 * k
-
-            def step(pos=pos, k=k):
-                for part in range(3):
+            for part in range(3):
+
+                def step(pos, k=k, part=part):
                     if k == (0 if part == 0 else 1):
                         self.loading(part, pos).wait()
                     if k > 0:
@@ -765,19 +764,20 @@
                     if k < STAGES:
                         for sends, _, copy, _ in self.moves(part, k, pos):
                             when(sends, lambda copy=copy: copy.start())
-                        continue
+                        return
                     self.finish(part, pos)
                     for stage in range(STAGES):
                         for sends, _, copy, _ in self.moves(part, stage, pos):
                             when(sends, lambda copy=copy: copy.wait_send())
 
-            if isinstance(pos, int):
+                pos = r - SCATTER_DELAY[part][k]
+                if not isinstance(r, int):
+                    pl.when(inside(pos, GROUPS - 1))(functools.partial(step, pos))
+                    continue
                 if 0 <= pos < GROUPS - 1:
-                    step()
-            else:
-                pl.when(inside(pos, GROUPS - 1))(step)
-            if isinstance(r, int) and r - AFTER == k:
-                step(AT, k)
+                    step(pos)
+                if r - AFTER == k:
+                    step(AT)
 
 
 def norm_back(v, gain, d):
@@ -1134,7 +1134,6 @@
 
     swap = small_to(small, 0, partner, 0)
     swap.start()
-    sc.round(10)
     fold_out.wait()
     for a in range(zs):
         for b in range(ys):
@@ -1143,24 +1142,24 @@
     fold_in.start()
     fold_in.wait()
     sc.start_load(AT)
-    sc.round(11)
+    sc.round(10)
     swap.wait()
     small[...] = small[...] + sland[0]
     swap = small_to(small, 1, here.dev(z, y, 1 - x), 1)
     swap.start()
-    sc.round(12)
+    sc.round(11)
     swap.wait()
     small[...] = small[...] + sland[1]
     swap = small_to(small, 2, here.dev(z, 1 - y, x), 2)
     swap.start()
-    sc.round(13)
+    sc.round(12)
     swap.wait()
     small[...] = small[...] + sland[2]
     swaps = []
     for far in range(1, zs):
         swaps.append(small_to(small, 3 + far, here.dev((z + far) % zs, y, x), 2 + far))
         swaps[-1].start()
-    sc.round(14)
+    sc.round(13)
     for swap in swaps:
         swap.wait()
     sland[3] = small[...]
@@ -1170,7 +1169,7 @@
     small[...] = ordered
     small_out = pltpu.make_async_copy(small, o_small, osem.at[3])
     small_out.start()
-    for r in range(15, GROUPS - 1 + 2 * STAGES):
+    for r in range(14, AFTER + STAGES + 1):
         sc.round(r)
     res_out = pltpu.make_async_copy(res, o_res, osem.at[4])
     res_out.start()

time: 425 us -> 408 us (0.960)
  Pallas kernels: 398 us -> 381 us
    pallas_call x1, Pallas kernels: 202 us -> 193 us  [forward_call(): pl.pallas_call(functools.partial(forward_kernel, n, heads), out_shape=(sh...]
    pallas_call x1, Pallas kernels: 197 us -> 188 us  [backward_call(): pl.pallas_call(functools.partial(backward_kernel, n, heads), out_shape=(s...]
where the time goes in v3:
time: 408 us; the launch traced here: 406 us
  Pallas kernels  381 us (93%)
  local copies, waits for them, and re-layouts  18.6 us (5%)
  other arithmetic  5.75 us (1%)
    pallas_call x1, Pallas kernels, forward_call(): pl.pallas_call(functools.partial(forward_kernel, n, heads), out_shape=(sh...  193 us
    pallas_call x1, Pallas kernels, backward_call(): pl.pallas_call(functools.partial(backward_kernel, n, heads), out_shape=(s...  188 us
    unnamed x20, local copies, waits for them, and re-layouts  12.4 us

profile of v3, /device:TPU:0, one launch (start us, length us, event | category | flops | bytes accessed | tf_op | source)
XLA Modules:
  0.0 406.5 jit_solution(6148996254816420074)
XLA Ops:
  0.6 0.0 copy-start.4
  0.7 1.3 broadcast_in_dim.91.na
  2.0 1.3 broadcast_in_dim.92.nf
  3.3 0.7 add_select_fusion.3
  4.0 0.8 reverse
  4.8 0.1 slice.48
  4.9 0.1 pad_bitcast_fusion
  4.9 0.6 pad.9.table
  5.6 0.0 copy-start.2
  5.6 1.5 copy.27.rel
  7.0 0.9 select_convert_fusion.qx
  8.0 1.7 select_convert_fusion.1.kx_own
  9.6 1.3 pad_maximum_fusion.1
  10.9 0.0 copy-done.4
  11.0 0.0 copy-start.3
  11.0 1.1 pad_maximum_fusion.slab
  12.1 0.0 copy-done.2
  12.1 1.6 copy.25.hid
  13.7 0.0 copy-done.3
  13.7 1.5 copy.26.dy
  15.2 193.0 %forward.1 = (bf16[8,4,2,2,48,1472]{5,4,3,2,1,0:T(8,128)(2,1)}, f32[1024,1472]{1,0:T(8,128)}, f32[1024,1472]{1,0:T(8,128)}, f32[512,1472]{1,0:T(8,128)}, f32[384...) custom-call(bf16[8,48,1472]{2,1,0:T(8,128)(2,1)} %pad_maximum_fusion, ...), custom_call_target="tpu_custom_call" | custom-call | flops 54999998464 | bytes 80000000 | tf_op jit(solution)/shard_map/forward/pallas_call | solution.py:563
  208.2 188.4 %backward.1 = (bf16[8,4,2,2,48,1472]{5,4,3,2,1,0:T(8,128)(2,1)}, bf16[512,1472]{1,0:T(8,128)(2,1)}, f32[512,1472]{1,0:T(8,128)}, f32[8,48,1472]{2,1,0:T(8,128)},...) custom-call(bf16[8,4,2,2,48,1472]{5,4,3,2,1,0:T(8,128)(2,1)} %get-tuple-eleme, ...), custom_call_target="tpu_custom_call", output_to_operand_aliasing={{0}: (0, {})} | custom-call | flops 12000000000 | bytes 60000000 | tf_op jit(solution)/shard_map/backward/pallas_call | solution.py:1190
  396.6 0.0 copy-start.5
  396.6 0.0 copy-start.1
  396.6 2.7 copy.31
  399.3 0.0 copy-done.5
  399.4 0.7 copy.33
  400.0 0.6 slice_bitcast_fusion.1
  400.6 0.0 copy-done.1
  400.6 0.7 slice_bitcast_fusion
  401.4 0.2 slice.31
  401.5 0.0 copy-start
  401.6 1.4 fusion.3
  402.9 1.3 copy-done
  404.2 2.3 copy.32
  (5 shorter events, 0.0 us)
Async XLA Ops:
  0.6 10.3 %copy-start.4 = (bf16[1472,48]{0,1:T(8,128)(2,1)S(1)}, bf16[1472,48]{0,1:T(8,128)(2,1)}, u32[]{:S(2)}) copy-start(bf16[1472,48]{0,1:T(8,128)(2,1)} %param.16) | copy-start | bytes 423940
  5.6 6.5 %copy-start.2 = (bf16[512,1472]{0,1:T(8,128)(2,1)S(1)}, bf16[512,1472]{0,1:T(8,128)(2,1)}, u32[]{:S(2)}) copy-start(bf16[512,1472]{0,1:T(8,128)(2,1)} %param.12) | copy-start | bytes 4521988
  11.0 2.7 copy-start.3
  396.6 2.7 copy-start.5
  396.6 4.0 copy-start.1
  401.5 2.6 copy-start

commit v4 on v3

--- a/solution.py
+++ b/solution.py
@@ -258,7 +258,7 @@
 
 def forward_kernel(
     n, heads,
-    slab, hid, dy, kx_own, qx, table, rel, na, nf,
+    slab, hid, dy, qx, table, rel, gains,
     o_grads, o_outp, o_dn2p, o_x1, o_at, o_q, o_kv, o_kx, o_lse, o_ga,
     G, ga, n2f, dyf, kv, kx, qv, x1, at, lse,
     gs, gr, lsem, hs, hr, ks, kr, cs, cr, osem, stsem,
@@ -288,7 +288,7 @@
     ]
     for copy in own:
         copy.start()
-    kx_in = pltpu.make_async_copy(kx_own, kx.at[centre], lsem.at[GROUPS])
+    kx_in = pltpu.make_async_copy(qx.at[:, 0:128], kx.at[centre], lsem.at[GROUPS])
     kx_in.start()
     dy_in = pltpu.make_async_copy(dy, dyf.at[mine], lsem.at[GROUPS + 1])
     dy_in.start()
@@ -319,7 +319,7 @@
         def norm_rows(i, _):
             at_rows = pl.ds(i * 64, 64)
             v = hid[at_rows, :].astype(F32)
-            n1[at_rows, :] = (v * row_norm(v) * na[...]).astype(BF)
+            n1[at_rows, :] = (v * row_norm(v) * gains[0:1, :]).astype(BF)
             return 0
 
         lax.fori_loop(0, rows // 64, norm_rows, 0)
@@ -399,7 +399,7 @@
                 head = hp * 2 + e
                 q = qv[pl.ds(base, 256), cols]
                 q = jnp.where(lane == e, q, jnp.zeros_like(q))
-                qa = jnp.concatenate([q, qx[pl.ds(base, 256), :]], 1)
+                qa = jnp.concatenate([q, qx[pl.ds(base, 256), 128:256]], 1)
 
                 def score(b, m):
                     at_rows = pl.ds(pl.multiple_of(base + b * 256, 256), 256)
@@ -454,7 +454,7 @@
             a = at[:, at_rows].T.astype(BF)
             v = hid[at_rows, :].astype(F32) + nn(a, w_out)
             x1[at_rows, :] = v
-            n2f[pl.ds(pl.multiple_of(c * rows + i * 128, 128), 128), :] = (v * row_norm(v) * nf[...]).astype(BF)
+            n2f[pl.ds(pl.multiple_of(c * rows + i * 128, 128), 128), :] = (v * row_norm(v) * gains[1:2, :]).astype(BF)
             return 0
 
         lax.fori_loop(0, rows // 128, after, 0)
@@ -483,6 +483,13 @@
     def feed(acc_o, acc_n, ft, gt, ut, stage):
         acc_o[...] = jnp.zeros_like(acc_o)
         acc_n[...] = jnp.zeros_like(acc_n)
+
+        def acc_out(i):
+            at_rows = pl.ds(pl.multiple_of(i * 256, 256), 256)
+            return (
+                pltpu.make_async_copy(acc_o.at[at_rows], o_outp.at[at_rows], osem.at[i]),
+                pltpu.make_async_copy(acc_n.at[at_rows], o_dn2p.at[at_rows], osem.at[4 + i]),
+            )
 
         def stage_out(j):
             return pltpu.make_async_copy(stage.at[j % 2], o_grads.at[j + 1], stsem.at[j % 2])
@@ -510,6 +517,12 @@
                 ut[:, at_rows] = du
                 acc_o[at_rows, :] += nn(f.T, whole(wd))
                 acc_n[at_rows, :] += nn(dg.T, whole(wg)) + nn(du.T, whole(wu))
+
+                @pl.when(j == GROUPS - 2)
+                def _():
+                    for o in acc_out(i):
+                        o.start()
+
                 return 0
 
             lax.fori_loop(0, 2 * rows // 256, tokens, 0, unroll=2)
@@ -526,15 +539,10 @@
             return 0
 
         lax.fori_loop(0, GROUPS - 1, chunk, 0)
-        outs = [
-            pltpu.make_async_copy(acc_o, o_outp, osem.at[0]),
-            pltpu.make_async_copy(acc_n, o_dn2p, osem.at[1]),
-        ]
-        for o in outs:
-            o.start()
         gather_drain(parts, copy)
-        for o in outs:
-            o.wait()
+        for i in range(2 * rows // 256):
+            for o in acc_out(i):
+                o.wait()
         stage_out(GROUPS - 3).wait()
         stage_out(GROUPS - 2).wait()
 
@@ -549,7 +557,7 @@
     )
 
 
-def forward_call(n, heads, slab, hid, dy, kx_own, qx, table, rel, na, nf):
+def forward_call(n, heads, slab, hid, dy, qx, table, rel, gains):
     rows, D = hid.shape
     inner = heads * 64
     zs, ys, xs = GRIDS[n]
@@ -574,7 +582,7 @@
             shape((8, rows), F32),
             shape((zs, ys, xs, 2, PIECE, D), BF),
         ),
-        in_specs=[any_, vm, any_, any_, vm, vm, sm, vm, vm],
+        in_specs=[any_, vm, any_, vm, vm, sm, vm],
         out_specs=(any_,) * 10,
         scratch_shapes=[
             pltpu.VMEM((GROUPS, zs, ys, xs, PIECE, D), BF),
@@ -598,7 +606,7 @@
         ),
         cost_estimate=pl.CostEstimate(flops=55 * 10**9, bytes_accessed=80 * 10**6, transcendentals=10**7),
         name="forward",
-    )(slab, hid, dy, kx_own, qx, table, rel, na, nf)
+    )(slab, hid, dy, qx, table, rel, gains)
 
 
 def prepare(hidden, segments, delete_mask, bucket_table, attn_weight, gate_weight, up_weight, down_weight):
@@ -608,17 +616,19 @@
     ffn = jnp.stack([gate_weight.T, up_weight.T, down_weight]).reshape(3, groups, 16, D)
     ffn = jnp.transpose(ffn, (1, 0, 2, 3)).reshape(groups, PIECE, D)
     slab = jnp.concatenate([attn_weight.T[None], ffn], 0)
-    lane = jnp.arange(128, dtype=jnp.int32)[None, :]
+    wide = jnp.arange(256, dtype=jnp.int32)[None, :]
+    lane = wide % 128
     seg = segments[:, None]
     digit = jnp.where(lane < 9, seg % 8, jnp.where(lane < 17, (seg // 8) % 8, seg // 64))
     hit = digit == (lane - 1) % 8
     coded = (lane >= 1) & (lane < 25)
-    kx = jnp.where(lane == 0, delete_mask.astype(F32)[:, None], jnp.where(coded & ~hit, -BIG, 0.0)).astype(BF)
-    qx = jnp.where((lane == 0) | (lane == 25) | (coded & hit), 1.0, 0.0).astype(BF)
+    key = jnp.where(lane == 0, delete_mask.astype(F32)[:, None], jnp.where(coded & ~hit, -BIG, 0.0))
+    query = jnp.where((lane == 0) | (lane == 25) | (coded & hit), 1.0, 0.0)
+    codes = jnp.where(wide < 128, key, query).astype(BF)
     reach = bucket_table.shape[0]
     table = jnp.pad(jnp.flip(bucket_table), (257, 20 * 128 - 257 - reach), constant_values=-1).reshape(20, 128)
     table = jnp.pad(table, ((0, 4), (0, 0)), constant_values=-1)
-    return slab, kx, qx, table
+    return slab, codes, table
 
 
 FIRST = (1, 2, 3, 4, 5, 6, 7, 0)
@@ -797,7 +807,7 @@
 def backward_kernel(
     n, heads,
     grads, outp, dn2p, x1_in, at_in, q_in, kv_in, kx_in, lse, ga_in,
-    hid, dy, qx, table, rel, na, nf,
+    hid, dy, qx, table, rel, gains,
     gr, o_out, o_dh, o_res, o_small, dn_land, op_land,
     work, land, landa, landz, res, dx1, kv, kx, qv, at, ga, dat, das, back, fold, small, sland,
     ss, rs, lds, cs, cr, hs, hr, ls, ps, pr, osem,
@@ -855,7 +865,7 @@
         def through(i, total):
             at_rows = pl.ds(pl.multiple_of(i * 128, 128), 128)
             d = dx1[at_rows, :] + other[at_rows, :]
-            back_v, gain_d = norm_back(x1[at_rows, :], nf[...], d)
+            back_v, gain_d = norm_back(x1[at_rows, :], gains[1:2, :], d)
             v = grad[at_rows, :].astype(F32) + back_v
             dx1[at_rows, :] = v
             v = v.astype(BF)
@@ -974,7 +984,7 @@
                 here_q = pl.ds(base, 256)
                 q = qv[here_q, cols]
                 q = jnp.where(lane == e, q, jnp.zeros_like(q))
-                qa = jnp.concatenate([q, qx[here_q, :]], 1)
+                qa = jnp.concatenate([q, qx[here_q, 128:256]], 1)
                 da = das[here_q, cols]
                 da = jnp.where(lane == e, da, jnp.zeros_like(da))
                 logs = lse[pl.ds(head, 1), here_q]
@@ -1052,7 +1062,7 @@
         def norm_rows(i, _):
             at_rows = pl.ds(pl.multiple_of(i * 64, 64), 64)
             v = hid_v[at_rows, :].astype(F32)
-            n1[at_rows, :] = (v * row_norm(v) * na[...]).astype(BF)
+            n1[at_rows, :] = (v * row_norm(v) * gains[0:1, :]).astype(BF)
             return 0
 
         lax.fori_loop(0, rows // 64, norm_rows, 0)
@@ -1093,7 +1103,7 @@
             d = nn(proj[at_rows, 0:inner], ga[0].reshape(inner, D))
             d = d + nn(proj[at_rows, inner : 2 * inner], ga[1].reshape(inner, D))
             d = d + nn(proj[at_rows, 2 * inner : 3 * inner], ga[2].reshape(inner, D))
-            back_v, gain_d = norm_back(hid_v[at_rows, :].astype(F32), na[...], d)
+            back_v, gain_d = norm_back(hid_v[at_rows, :].astype(F32), gains[0:1, :], d)
             dx1[at_rows, :] = dx1[at_rows, :] + back_v
             return total + jnp.sum(gain_d.reshape(16, 8, D), axis=0)
 
@@ -1177,7 +1187,7 @@
     small_out.wait()
 
 
-def backward_call(n, heads, kept, hid, dy, qx, table, rel, na, nf):
+def backward_call(n, heads, kept, hid, dy, qx, table, rel, gains):
     grads, outp, dn2p, x1, at, q, kv, kx, lse, ga = kept
     rows, D = hid.shape
     inner = heads * 64
@@ -1198,7 +1208,7 @@
             shape((rows, D), F32),
             shape((rows, D), F32),
         ),
-        in_specs=[any_] * 8 + [vm] + [any_] * 3 + [vm, vm, sm, vm, vm],
+        in_specs=[any_] * 8 + [vm] + [any_] * 3 + [vm, vm, sm, vm],
         out_specs=(any_,) * 7,
         input_output_aliases={0: 0},
         scratch_shapes=[
@@ -1231,7 +1241,7 @@
         ),
         cost_estimate=pl.CostEstimate(flops=12 * 10**9, bytes_accessed=60 * 10**6, transcendentals=10**7),
         name="backward",
-    )(grads, outp, dn2p, x1, at, q, kv, kx, lse, ga, hid, dy, qx, table, rel, na, nf)
+    )(grads, outp, dn2p, x1, at, q, kv, kx, lse, ga, hid, dy, qx, table, rel, gains)
 
 
 def shards(
@@ -1240,13 +1250,13 @@
 ):
     heads = rel_bias.shape[1]
     D = hidden.shape[1]
-    slab, kx, qx, table = prepare(
+    slab, qx, table = prepare(
         hidden, segments, delete_mask, bucket_table, attn_weight, gate_weight, up_weight, down_weight
     )
-    na, nf = norm_attn[None], norm_ffn[None]
-    kept = forward_call(n, heads, slab, hidden, out_grad, kx, qx, table, rel_bias, na, nf)
+    gains = jnp.stack([norm_attn, norm_ffn])
+    kept = forward_call(n, heads, slab, hidden, out_grad, qx, table, rel_bias, gains)
     _, output, d_hidden, res, small, _, _ = backward_call(
-        n, heads, kept, hidden, out_grad, qx, table, rel_bias, na, nf
+        n, heads, kept, hidden, out_grad, qx, table, rel_bias, gains
     )
     ffn = res[1:].reshape(GROUPS - 1, 3, 16, D)
     mats = [ffn[:, i].reshape(-1, D) for i in range(3)]

time: 408 us -> 403 us (0.988)
  no operation moved by 1% of the time
where the time goes in v4:
time: 403 us; the launch traced here: 401 us
  Pallas kernels  378 us (94%)
  local copies, waits for them, and re-layouts  17.4 us (4%)
  other arithmetic  5.5 us (1%)
    pallas_call x1, Pallas kernels, forward_call(): pl.pallas_call(functools.partial(forward_kernel, n, heads), out_shape=(sh...  189 us
    pallas_call x1, Pallas kernels, backward_call(): pl.pallas_call(functools.partial(backward_kernel, n, heads), out_shape=(s...  188 us
    unnamed x20, local copies, waits for them, and re-layouts  12.4 us

profile of v4, /device:TPU:0, one launch (start us, length us, event | category | flops | bytes accessed | tf_op | source)
XLA Modules:
  0.0 401.2 jit_solution(13874063488438433894)
XLA Ops:
  0.6 0.0 copy-start.4
  0.7 0.7 stack.25
  1.4 0.7 stack.26
  2.1 0.6 pad_maximum_fusion.2.gains
  2.8 0.7 add_select_fusion.3
  3.5 0.8 reverse
  4.2 0.1 slice.48
  4.3 0.1 pad_bitcast_fusion
  4.4 0.6 pad.9.table
  5.0 0.0 copy-start.2
  5.0 1.5 copy.27.rel
  6.5 1.7 select_convert_fusion.qx
  8.2 1.3 pad_maximum_fusion.1
  9.5 0.0 copy-done.4
  9.5 0.0 copy-start.3
  9.5 1.1 pad_maximum_fusion.slab
  10.7 0.0 copy-done.2
  10.7 1.6 copy.25.hid
  12.2 0.0 copy-done.3
  12.2 1.5 copy.26.dy
  13.8 189.2 %forward.1 = (bf16[8,4,2,2,48,1472]{5,4,3,2,1,0:T(8,128)(2,1)}, f32[1024,1472]{1,0:T(8,128)}, f32[1024,1472]{1,0:T(8,128)}, f32[512,1472]{1,0:T(8,128)}, f32[384...) custom-call(bf16[8,48,1472]{2,1,0:T(8,128)(2,1)} %pad_maximum_fusion, ...), custom_call_target="tpu_custom_call" | custom-call | flops 54999998464 | bytes 80000000 | tf_op jit(solution)/shard_map/forward/pallas_call | solution.py:571
  203.0 188.3 %backward.1 = (bf16[8,4,2,2,48,1472]{5,4,3,2,1,0:T(8,128)(2,1)}, bf16[512,1472]{1,0:T(8,128)(2,1)}, f32[512,1472]{1,0:T(8,128)}, f32[8,48,1472]{2,1,0:T(8,128)},...) custom-call(bf16[8,4,2,2,48,1472]{5,4,3,2,1,0:T(8,128)(2,1)} %get-tuple-eleme, ...), custom_call_target="tpu_custom_call", output_to_operand_aliasing={{0}: (0, {})} | custom-call | flops 12000000000 | bytes 60000000 | tf_op jit(solution)/shard_map/backward/pallas_call | solution.py:1200
  391.3 0.0 copy-start.5
  391.3 0.0 copy-start.1
  391.4 2.7 copy.31
  394.1 0.0 copy-done.5
  394.1 0.7 copy.33
  394.7 0.6 slice_bitcast_fusion.1
  395.3 0.0 copy-done.1
  395.4 0.7 slice_bitcast_fusion
  396.1 0.2 slice.31
  396.3 0.0 copy-start
  396.3 1.4 fusion.3
  397.6 1.3 copy-done
  398.9 2.3 copy.32
  (5 shorter events, 0.0 us)
Async XLA Ops:
  0.6 8.9 %copy-start.4 = (bf16[1472,48]{0,1:T(8,128)(2,1)S(1)}, bf16[1472,48]{0,1:T(8,128)(2,1)}, u32[]{:S(2)}) copy-start(bf16[1472,48]{0,1:T(8,128)(2,1)} %param.16) | copy-start | bytes 423940
  5.0 5.7 %copy-start.2 = (bf16[512,1472]{0,1:T(8,128)(2,1)S(1)}, bf16[512,1472]{0,1:T(8,128)(2,1)}, u32[]{:S(2)}) copy-start(bf16[512,1472]{0,1:T(8,128)(2,1)} %param.12) | copy-start | bytes 4521988
  9.5 2.7 copy-start.3
  391.3 2.7 copy-start.5
  391.3 4.0 copy-start.1
  396.3 2.6 copy-start
